TPU v7x, 256 devices: a whole 4x4x8 slice. The times are simulated.
256 devices in a mesh: sec: 4 (over y), dom: 64 (over x, z, core).
Axes of the slice: x: 4, y: 4, z: 8, core: 2. Of those that a mesh axis runs over, the one named last changes fastest.
Arguments:
- defect: float32 [5, 64, 16, 8192], P(None, None, 'sec', 'dom'), may hold values from -6 to 6
- point_inverse: float32 [5, 5, 64, 16, 8192], P(None, None, None, 'sec', 'dom'), may hold values from -0.04 to 0.25
- flux_jacobian: float32 [3, 5, 5, 16, 8192], P(None, None, None, 'sec', 'dom'), may hold values from -1 to 1
- time_term: float32 [16, 8192], P('sec', 'dom'), may hold values from 2 to 4
- penalty: float32 [3, 16, 8192], P(None, 'sec', 'dom'), may hold values from 0.5 to 2
- element_inverse: float32 [5, 5, 16, 8192], P(None, None, 'sec', 'dom'), may hold values from -0.04 to 0.25
Outputs:
- correction: float32 [5, 64, 16, 8192], P(None, None, 'sec', 'dom')
All inputs are finite; a program needn't handle non-finite values.
Results may differ from a plain program's by a relative error of at most 0.0001.
Values sent between devices are 32-bit elements; how exact they have to be, the bound alone decides.
A program may use at most 64 MiB of HBM per device.

v0:
```python
import jax
import jax.numpy as jnp
import numpy as np
from jax import lax
from jax.experimental import pallas as pl
from jax.experimental.pallas import tpu as pltpu
from jax.sharding import PartitionSpec as P

EZ = 32
DAMPING = 0.7
MESH = pl.DeviceIdType.MESH
F32 = jnp.float32

STEPS = ((1, 0), (-1, 0), (0, 1), (0, -1), (1, 1), (1, -1), (-1, 1), (-1, -1))
RIGHT, LEFT, UP, DOWN, RIGHT_UP, RIGHT_DOWN, LEFT_UP, LEFT_DOWN = range(8)


def node_tables():
    points = np.array([-1.0, -1.0 / np.sqrt(5.0), 1.0 / np.sqrt(5.0), 1.0])
    barycentric = np.array(
        [1.0 / np.prod([points[j] - points[k] for k in range(4) if k != j]) for j in range(4)]
    )
    derivative = np.zeros((4, 4))
    for i in range(4):
        for j in range(4):
            if i != j:
                derivative[i, j] = barycentric[j] / barycentric[i] / (points[i] - points[j])
        derivative[i, i] = -np.sum(derivative[i])
    return derivative, (1.0 - points[1]) / 2.0, (1.0 + points[1]) / 2.0


DERIVATIVE, NEAR, FAR = node_tables()
EVEN = [float((DERIVATIVE[i, 0] + DERIVATIVE[i, 3]) / 2.0) for i in (0, 1)]
ODD = [[float((DERIVATIVE[i, j] - DERIVATIVE[i, 3 - j]) / 2.0) for j in (0, 1)] for i in (0, 1)]
NEAR, FAR = float(NEAR), float(FAR)


def roll_lanes(value, shift):
    shift %= 128
    return value if shift == 0 else pltpu.roll(value, shift, value.ndim - 1)


def roll_rows(value, shift):
    shift %= 8
    return value if shift == 0 else pltpu.roll(value, shift, value.ndim - 2)


def line_slopes(u0, u1, u2, u3):
    outer, inner = u0 - u3, u1 - u2
    even = (u0 + u3) - (u1 + u2)
    e0, e1 = EVEN[0] * even, EVEN[1] * even
    o0 = ODD[0][0] * outer + ODD[0][1] * inner
    o1 = ODD[1][0] * outer + ODD[1][1] * inner
    return o0 + e0, o1 + e1, o1 - e1, o0 - e0


def kernel(
    sec_count, dom_count,
    s_ref, b_ref, j_ref, t_ref, p_ref, e_ref,
    x_ref,
    jd, own, dg, res, sly, slz,
    fsend, frecv, ssend, srecv, esend, erecv, dsend, drecv, dssend, dsrecv,
    wst, wm, ws, wres, wsl, wc, wrx, wry, wb, fin,
    f_ss, f_rs, s_ss, s_rs, e_ss, e_rs,
):
    me_sec, me_dom = lax.axis_index("sec"), lax.axis_index("dom")
    has_dom = {0: None, 1: me_dom < dom_count - 1, -1: me_dom > 0}
    has_sec = {0: None, 1: me_sec < sec_count - 1, -1: me_sec > 0}

    def exists(dx, dy):
        a, b = has_dom[dx], has_sec[dy]
        if a is None:
            return b
        if b is None:
            return a
        return jnp.logical_and(a, b)

    def target(direction):
        dx, dy = STEPS[direction]
        return (me_sec + dy, me_dom + dx)

    barrier = pltpu.get_barrier_semaphore()
    for direction in range(8):
        @pl.when(exists(*STEPS[direction]))
        def _(direction=direction):
            pl.semaphore_signal(barrier, inc=1, device_id=target(direction), device_id_type=MESH)
    one, zero = jnp.int32(1), jnp.int32(0)
    across = jnp.where(me_dom < dom_count - 1, one, zero) + jnp.where(me_dom > 0, one, zero) + 1
    along = jnp.where(me_sec < sec_count - 1, one, zero) + jnp.where(me_sec > 0, one, zero) + 1

    def copy(direction, src, dst, send_sem, recv_sem):
        return pltpu.make_async_remote_copy(
            src_ref=src, dst_ref=dst, send_sem=send_sem, recv_sem=recv_sem,
            device_id=target(direction), device_id_type=MESH,
        )

    def send(direction, src, dst, send_sem, recv_sem):
        @pl.when(exists(*STEPS[direction]))
        def _():
            copy(direction, src, dst, send_sem, recv_sem).start()

    def sent(direction, src, dst, send_sem, recv_sem):
        @pl.when(exists(*STEPS[direction]))
        def _():
            copy(direction, src, dst, send_sem, recv_sem).wait_send()

    def arrived(direction, src, dst, send_sem, recv_sem):
        dx, dy = STEPS[direction]

        @pl.when(exists(-dx, -dy))
        def _():
            copy(direction, src, dst, send_sem, recv_sem).wait_recv()

    def clear(direction, dst):
        dx, dy = STEPS[direction]

        @pl.when(jnp.logical_not(exists(-dx, -dy)))
        def _():
            dst[...] = jnp.zeros_like(dst)

    def fine_message(stage, direction):
        return (direction, fsend.at[stage, direction], frecv.at[stage, direction],
                f_ss.at[stage, direction], f_rs.at[stage, direction])

    def static_message(direction):
        if direction < 4:
            src, dst = ssend.at[direction], srecv.at[direction]
        else:
            src, dst = dssend.at[direction - 4], dsrecv.at[direction - 4]
        return direction, src, dst, s_ss.at[direction], s_rs.at[direction]

    def coarse_message(stage, direction):
        if direction < 4:
            src, dst = esend.at[stage, direction], erecv.at[stage, direction]
        else:
            src, dst = dsend.at[stage, direction - 4], drecv.at[stage, direction - 4]
        return direction, src, dst, e_ss.at[stage, direction], e_rs.at[stage, direction]

    lane = lax.broadcasted_iota(jnp.int32, (8, 128), 1)
    row = lax.broadcasted_iota(jnp.int32, (8, 128), 0)
    low_half = row < 4
    low_lanes = lane < 64
    z_index = lane % EZ
    has_next = jnp.where(z_index < EZ - 1, 1.0, 0.0)
    has_prior = jnp.where(z_index > 0, 1.0, 0.0)
    lower = jnp.where(low_half, 1.0, 0.0)
    upper = 1.0 - lower

    def halves(a, b):
        return jnp.where(low_half, F32(a), F32(b))

    for array, start, count, scale in ((j_ref, 0, 75, 0.5), (e_ref, 75, 25, DAMPING)):
        def spread(n, c, array=array, start=start, scale=scale):
            value = array[n]
            jd[start + n, 0:4] = value
            jd[start + n, 4:8] = value
            own[start + n] = scale * jd[start + n]
            return c
        lax.fori_loop(0, count, spread, 0)
    for n, value in enumerate((t_ref[...], p_ref[0], p_ref[1], p_ref[2])):
        own[100 + n, 0:4] = value
        own[100 + n, 4:8] = value
    time, pen_x, pen_y, pen_z = own[100], own[101], own[102], own[103]
    for f in range(2):
        for q in range(8):
            j, k2 = q // 2, q % 2
            total = time + pen_z * (lower if k2 == 0 else upper)
            if j in (0, 3):
                total = total + pen_y
            dg[f, q] = total + pen_x if f else total

    px_prior = jnp.where(lane >= EZ, pen_x, 0.0)
    px_next = jnp.where(lane < 128 - EZ, pen_x, 0.0)
    px_left = jnp.where(lane < EZ, pen_x, 0.0)
    px_right = jnp.where(lane >= 128 - EZ, pen_x, 0.0)
    row4 = row % 4
    py_prior = jnp.where(row4 != 0, pen_y, 0.0)
    py_next = jnp.where(row4 != 3, pen_y, 0.0)
    py_below = jnp.where(row4 == 0, pen_y, 0.0)
    py_above = jnp.where(row4 == 3, pen_y, 0.0)
    pz_prior = pen_z * lower * has_prior
    pz_next = pen_z * upper * has_next

    def smooth(source, first):
        def block(q, c):
            values = [source[a, :, q] for a in range(5)]
            for a in range(5):
                total = b_ref[a, 0, :, q] * values[0]
                for b in range(1, 5):
                    total = total + b_ref[a, b, :, q] * values[b]
                total = DAMPING * total
                x_ref[a, :, q] = total if first else x_ref[a, :, q] + total
            return c
        lax.fori_loop(0, 8, block, 0)

    def send_faces(stage):
        def pieces(face, rolled, place):
            packed = None
            for m in range(4):
                piece = rolled(face(m), m)
                packed = piece if packed is None else jnp.where(place == m, piece, packed)
            return packed

        def one_variable(a, c):
            fsend[stage, RIGHT, a] = pieces(
                lambda m: x_ref[a, 3, 2 * m:2 * m + 2], lambda v, m: roll_lanes(v, EZ * (m + 1)), lane // EZ)
            fsend[stage, LEFT, a] = pieces(
                lambda m: x_ref[a, 0, 2 * m:2 * m + 2], lambda v, m: roll_lanes(v, EZ * m), lane // EZ)
            fsend[stage, UP, a] = pieces(
                lambda m: x_ref[a, m, 6:8], lambda v, m: roll_rows(v, m - 3), row4)
            fsend[stage, DOWN, a] = pieces(
                lambda m: x_ref[a, m, 0:2], lambda v, m: roll_rows(v, m), row4)
            return c
        lax.fori_loop(0, 5, one_variable, 0)
        for direction in range(4):
            send(*fine_message(stage, direction))

    even_z = halves(EVEN[0], -EVEN[1])
    even_z_swapped = halves(EVEN[1], -EVEN[0])
    odd_z = halves(ODD[0][0], ODD[1][1])
    odd_z_cross = halves(ODD[0][1], ODD[1][0])
    odd_z_swapped = halves(ODD[1][1], ODD[0][0])
    odd_z_cross_swapped = halves(ODD[1][0], ODD[0][1])

    def residual():
        def slab(n, c):
            a, i = n // 4, n % 4
            face = 1 - ((i + 1) // 2) % 2
            u = x_ref[a, i]
            r = s_ref[a, i] - dg[face] * u
            pairs = u.reshape(4, 2, 8, 128)
            v0, v1 = pairs[:, 0], pairs[:, 1]
            w0, w1 = roll_rows(v0, 4), roll_rows(v1, 4)
            even = (v0 + w1) - (w0 + v1)
            outer, inner = v0 - w1, w0 - v1
            z0 = odd_z * outer + odd_z_cross * inner + even_z * even
            z1 = odd_z_swapped * inner + odd_z_cross_swapped * outer - even_z_swapped * even
            slz[a, i] = jnp.stack([z0, z1], axis=1).reshape(8, 8, 128)
            add0 = pz_prior * roll_lanes(w1, 1)
            add1 = pz_next * roll_lanes(w0, -1)
            r = r + jnp.stack([add0, add1], axis=1).reshape(8, 8, 128)
            y = line_slopes(u[0:2], u[2:4], u[4:6], u[6:8])
            sly[a, i] = jnp.concatenate(y, axis=0)
            first = r[0:2] + py_prior * roll_rows(u[6:8], 1)
            last = r[6:8] + py_next * roll_rows(u[0:2], -1)
            res[a, i] = jnp.concatenate([first, r[2:6], last], axis=0)
            return c
        lax.fori_loop(0, 20, slab, 0)

        def block(q, c):
            total, slopes = [], []
            for a in range(5):
                u = x_ref[a, :, q]
                r = res[a, :, q]
                first = r[0] + px_prior * roll_lanes(u[3], EZ)
                last = r[3] + px_next * roll_lanes(u[0], -EZ)
                total.append(jnp.stack([first, r[1], r[2], last]))
                slopes.append(jnp.stack(line_slopes(u[0], u[1], u[2], u[3])))
            for d in range(3):
                if d == 1:
                    slopes = [sly[a, :, q] for a in range(5)]
                if d == 2:
                    slopes = [slz[a, :, q] for a in range(5)]
                for a in range(5):
                    for b in range(5):
                        total[a] = total[a] - jd[d * 25 + a * 5 + b] * slopes[b]
            for a in range(5):
                res[a, :, q] = total[a]
            return c
        lax.fori_loop(0, 8, block, 0)

    def add_halo(stage):
        for direction in range(4):
            arrived(*fine_message(stage, direction))

        def one_variable(a, c):
            from_left, from_right = frecv[stage, RIGHT, a], frecv[stage, LEFT, a]
            from_below, from_above = frecv[stage, UP, a], frecv[stage, DOWN, a]
            for m in range(4):
                q = slice(2 * m, 2 * m + 2)
                res[a, 0, q] = res[a, 0, q] + px_left * roll_lanes(from_left, -EZ * m)
                res[a, 3, q] = res[a, 3, q] + px_right * roll_lanes(from_right, 128 - EZ * (m + 1))
            for m in range(4):
                res[a, m, 0:2] = res[a, m, 0:2] + py_below * roll_rows(from_below, -m)
                res[a, m, 6:8] = res[a, m, 6:8] + py_above * roll_rows(from_above, 3 - m)
            return c
        lax.fori_loop(0, 5, one_variable, 0)

    def pack_columns(value, first_block):
        quarter = value.shape[0] // 4
        packed = None
        for m in range(4):
            piece = roll_rows(roll_lanes(value[m * quarter:(m + 1) * quarter], 64 * (m % 2)), 4 * (m // 2))
            place = jnp.logical_and(row // 4 == m // 2, lane // 64 == (first_block + m) % 2)
            packed = piece if packed is None else jnp.where(place, piece, packed)
        return packed

    def pack_rows(value, first_pair):
        quarter = value.shape[0] // 4
        packed = None
        for m in range(4):
            piece = roll_rows(value[m * quarter:(m + 1) * quarter], 2 * m)
            packed = piece if packed is None else jnp.where(row // 2 == (first_pair + m) % 4, piece, packed)
        return packed

    def pack_corner(rows_packed, keep_low):
        half = rows_packed.shape[0] // 2
        return jnp.where(low_lanes == keep_low, rows_packed[:half], roll_lanes(rows_packed[half:], 64))

    def unpack_columns(from_right, from_left):
        out = []
        for m in range(4):
            both = jnp.where(lane // 64 == m % 2, from_right, from_left)
            out.append(roll_rows(roll_lanes(both, -64 * (m % 2)), -4 * (m // 2)))
        return out

    def unpack_rows(from_above, from_below):
        return [roll_rows(jnp.where(row // 2 == m, from_above, from_below), 4 - 2 * m) for m in range(4)]

    def unpack_corner(right, left):
        return jnp.concatenate(
            [jnp.where(low_lanes, right, left), roll_lanes(jnp.where(low_lanes, left, right), 64)], axis=0)

    def fill_window(window, mine, columns, rows, corners):
        quarter = mine.shape[0] // 4
        side = unpack_columns(columns[0], columns[1])
        ends = unpack_rows(rows[0], rows[1])
        above = unpack_corner(corners[0], corners[1])
        below = unpack_corner(corners[2], corners[3])
        edge = unpack_rows(above, below)
        for m in range(4):
            part = slice(m * quarter, (m + 1) * quarter)
            window[0, part] = jnp.where(low_half, mine[part], ends[m])
            window[1, part] = jnp.where(low_half, side[m], edge[m])

    smooth(s_ref, True)
    pl.semaphore_wait(barrier, across * along - 1)
    send_faces(0)

    coefficients = own[...]
    ssend[RIGHT] = pack_columns(coefficients, 1)
    ssend[LEFT] = pack_columns(coefficients, 0)
    ssend[UP] = pack_rows(coefficients, 1)
    ssend[DOWN] = pack_rows(coefficients, 0)
    for direction, source, keep_low in (
        (RIGHT_UP, UP, False), (RIGHT_DOWN, DOWN, False), (LEFT_UP, UP, True), (LEFT_DOWN, DOWN, True)
    ):
        dssend[direction - 4] = pack_corner(ssend[source], keep_low)
    for direction in range(8):
        send(*static_message(direction))
    for stage in range(3):
        for direction in range(4):
            clear(direction, frecv.at[stage, direction])
    for stage in range(2):
        for direction in range(4):
            clear(direction, erecv.at[stage, direction])
        for direction in range(4, 8):
            clear(direction, drecv.at[stage, direction - 4])
    for direction in range(4):
        clear(direction, srecv.at[direction])
    for direction in range(4, 8):
        clear(direction, dsrecv.at[direction - 4])

    residual()
    add_halo(0)
    smooth(res, False)
    send_faces(1)
    residual()
    for direction in range(8):
        arrived(*static_message(direction))
    fill_window(
        wst, own,
        (srecv[LEFT], srecv[RIGHT]), (srecv[DOWN], srecv[UP]),
        (dsrecv[LEFT_DOWN - 4], dsrecv[RIGHT_DOWN - 4], dsrecv[LEFT_UP - 4], dsrecv[RIGHT_UP - 4]),
    )
    add_halo(1)

    near_low, far_low = halves(1.0, NEAR), halves(FAR, 0.0)
    near_high, far_high = halves(NEAR, 1.0), halves(0.0, FAR)

    def restrict(a, c):
        for ip in range(2):
            if ip == 0:
                x = res[a, 0] + NEAR * res[a, 1] + FAR * res[a, 2]
            else:
                x = FAR * res[a, 1] + NEAR * res[a, 2] + res[a, 3]
            for jp in range(2):
                if jp == 0:
                    y = x[0:2] + NEAR * x[2:4] + FAR * x[4:6]
                else:
                    y = FAR * x[2:4] + NEAR * x[4:6] + x[6:8]
                z0 = near_low * y[0] + far_low * y[1]
                z1 = far_high * y[0] + near_high * y[1]
                n = a * 8 + ip * 4 + jp * 2
                fin[n] = z0 + roll_rows(z0, 4)
                fin[n + 1] = z1 + roll_rows(z1, 4)
        return c
    lax.fori_loop(0, 5, restrict, 0)

    def exchange(stage, field, faces):
        nodes = faces.reshape(5, 2, 2, 2, 8, 128)
        x_low, x_up = nodes[:, 0].reshape(20, 8, 128), nodes[:, 1].reshape(20, 8, 128)
        y_low, y_up = nodes[:, :, 0].reshape(20, 8, 128), nodes[:, :, 1].reshape(20, 8, 128)
        esend[stage, RIGHT, 0:10] = pack_columns(field, 1)
        esend[stage, RIGHT, 10:15] = pack_columns(roll_lanes(x_up, EZ), 1)
        esend[stage, LEFT, 0:10] = pack_columns(field, 0)
        esend[stage, LEFT, 10:15] = pack_columns(roll_lanes(x_low, -EZ), 0)
        esend[stage, UP, 0:10] = pack_rows(field, 1)
        esend[stage, UP, 10:15] = pack_rows(roll_rows(y_up, 1), 1)
        esend[stage, DOWN, 0:10] = pack_rows(field, 0)
        esend[stage, DOWN, 10:15] = pack_rows(roll_rows(y_low, -1), 0)
        for direction, source, keep_low in (
            (RIGHT_UP, UP, False), (RIGHT_DOWN, DOWN, False), (LEFT_UP, UP, True), (LEFT_DOWN, DOWN, True)
        ):
            dsend[stage, direction - 4] = pack_corner(esend[stage, source, 0:10], keep_low)
        for direction in (4, 5, 6, 7, 0, 1, 2, 3):
            send(*coarse_message(stage, direction))

    def receive(stage, window, field):
        for direction in range(8):
            arrived(*coarse_message(stage, direction))
        fill_window(
            window, field,
            (erecv[stage, LEFT, 0:10], erecv[stage, RIGHT, 0:10]),
            (erecv[stage, DOWN, 0:10], erecv[stage, UP, 0:10]),
            (drecv[stage, LEFT_DOWN - 4], drecv[stage, RIGHT_DOWN - 4],
             drecv[stage, LEFT_UP - 4], drecv[stage, RIGHT_UP - 4]),
        )
        side = unpack_columns(erecv[stage, LEFT, 10:15], erecv[stage, RIGHT, 10:15])
        ends = unpack_rows(erecv[stage, DOWN, 10:15], erecv[stage, UP, 10:15])
        for m in range(4):
            wrx[5 * m:5 * m + 5] = side[m]
            wry[5 * m:5 * m + 5] = ends[m]

    strip_right = jnp.logical_and(low_half, lane // EZ == 1)
    strip_left = jnp.logical_and(low_half, lane // EZ == 2)

    def across_x(low0, low1, up0, up1, strip):
        l0, l1 = roll_lanes(low0, -EZ), roll_lanes(low1, -EZ)
        u0, u1 = roll_lanes(up0, EZ), roll_lanes(up1, EZ)
        not_last, first = lane < 128 - EZ, lane < EZ
        next0, next1 = jnp.where(not_last, l0, l1), jnp.where(not_last, l1, l0)
        prior0, prior1 = jnp.where(first, u1, u0), jnp.where(first, u0, u1)
        if strip is not None:
            next1 = jnp.where(strip_right, strip, next1)
            prior1 = jnp.where(strip_left, strip, prior1)
        return (next0, next1), (prior0, prior1)

    def window_faces(a, use_strips):
        tiles = [wm[tile, pl.ds(a * 8, 8)] for tile in range(2)]
        nodes = [u.reshape(2, 2, 2, 8, 128) for u in tiles]
        x_low, x_up = [u[0].reshape(4, 8, 128) for u in nodes], [u[1].reshape(4, 8, 128) for u in nodes]
        y_low, y_up = [u[:, 0].reshape(4, 8, 128) for u in nodes], [u[:, 1].reshape(4, 8, 128) for u in nodes]
        z_low, z_up = [u[:, :, 0].reshape(4, 8, 128) for u in nodes], [u[:, :, 1].reshape(4, 8, 128) for u in nodes]
        x_next, x_prior = across_x(
            x_low[0], x_low[1], x_up[0], x_up[1], wrx[pl.ds(a * 4, 4)] if use_strips else None)
        out = []
        for tile in range(2):
            px, py, pz = wst[tile, 101], wst[tile, 102], wst[tile, 103]
            x = (px * (x_low[tile] - x_prior[tile]), px * (x_up[tile] - x_next[tile]))
            y_next, y_prior = roll_rows(y_low[tile], -1), roll_rows(y_up[tile], 1)
            if tile == 0 and use_strips:
                strip = wry[pl.ds(a * 4, 4)]
                y_next = jnp.where(row == 5, strip, y_next)
                y_prior = jnp.where(row == 6, strip, y_prior)
            y = (py * (y_low[tile] - y_prior), py * (y_up[tile] - y_next))
            z = (pz * (z_low[tile] - has_prior * roll_lanes(z_up[tile], 1)),
                 pz * (z_up[tile] - has_next * roll_lanes(z_low[tile], -1)))
            slopes = (x_up[tile] - x_low[tile], y_up[tile] - y_low[tile], z_up[tile] - z_low[tile])
            out.append((tiles[tile], x, y, z, slopes))
        return out

    def fluxes(tiles):
        def one(n, c):
            d, tile = n // tiles, n % tiles
            slopes = [wsl[tile, d, b] for b in range(5)]
            for a in range(5):
                total = wst[tile, d * 25 + a * 5] * slopes[0]
                for b in range(1, 5):
                    total = total + wst[tile, d * 25 + a * 5 + b] * slopes[b]
                wc[tile, d, a] = total
            return c
        lax.fori_loop(0, 3 * tiles, one, 0)

    def middle_residual(use_strips):
        def one(a, c):
            for tile, (u, x, y, z, slopes) in enumerate(window_faces(a, use_strips)):
                r = ws[tile, pl.ds(a * 8, 8)] - wst[tile, 100] * u
                r = r.reshape(2, 2, 2, 8, 128)
                r = r - jnp.stack(x, axis=0).reshape(2, 2, 2, 8, 128)
                r = r - jnp.stack([v.reshape(2, 2, 8, 128) for v in y], axis=1)
                r = r - jnp.stack([v.reshape(2, 2, 8, 128) for v in z], axis=2)
                wres[tile, a] = r.reshape(8, 8, 128)
                for d in range(3):
                    wsl[tile, d, a] = slopes[d]
            return c
        lax.fori_loop(0, 5, one, 0)
        fluxes(2)

    def full_residual(tile, ip, a):
        r = wres[tile, a, pl.ds(ip * 4, 4)].reshape(2, 2, 8, 128)
        r = r - wc[tile, 0, a].reshape(2, 2, 8, 128)
        r = r - wc[tile, 1, a, pl.ds(ip * 2, 2)][None]
        return r - wc[tile, 2, a, pl.ds(ip * 2, 2)][:, None]

    def middle_sweep(use_strips):
        middle_residual(use_strips)

        def one(n, c):
            tile, ip = n // 2, n % 2
            r = [full_residual(tile, ip, a).reshape(4, 8, 128) for a in range(5)]
            for a in range(5):
                part = pl.ds(a * 8 + ip * 4, 4)
                total = wm[tile, part]
                for b in range(5):
                    total = total + wst[tile, 75 + a * 5 + b] * r[b]
                wm[tile, part] = total
            return c
        lax.fori_loop(0, 4, one, 0)

    def element_product(tile, values):
        out = []
        for a in range(5):
            total = wst[tile, 75 + a * 5] * values[0]
            for b in range(1, 5):
                total = total + wst[tile, 75 + a * 5 + b] * values[b]
            out.append(total)
        return out

    def own_guess(n, c):
        part = [fin[pl.ds(b * 8 + n * 4, 4)] for b in range(5)]
        for a, value in enumerate(element_product(0, part)):
            fin[pl.ds(40 + a * 8 + n * 4, 4)] = value
        return c
    lax.fori_loop(0, 2, own_guess, 0)
    exchange(0, fin[0:40], fin[40:80])
    receive(0, ws, fin[0:40])

    def first_guess(n, c):
        tile, ip = n // 2, n % 2
        part = [ws[tile, pl.ds(b * 8 + ip * 4, 4)] for b in range(5)]
        for a, value in enumerate(element_product(tile, part)):
            wm[tile, pl.ds(a * 8 + ip * 4, 4)] = value
        return c
    lax.fori_loop(0, 4, first_guess, 0)
    middle_sweep(True)
    middle_residual(False)

    for tile in range(2):
        def bottom_source(a, c, tile=tile):
            total = full_residual(tile, 0, a) + full_residual(tile, 1, a)
            total = total[0] + total[1]
            wb[0, tile, a] = total[0] + total[1]
            return c
        lax.fori_loop(0, 5, bottom_source, 0)
    for tile in range(2):
        values = [wb[0, tile, a] for a in range(5)]
        for a, value in enumerate(element_product(tile, values)):
            wb[1, tile, a] = value
    bottom = wb[1, 0]
    (x_next, _), (x_prior, _) = across_x(bottom, wb[1, 1], bottom, wb[1, 1], None)
    applied = (time + 2.0 * (pen_x + pen_y + pen_z)) * bottom
    applied = applied - pen_x * (x_next + x_prior)
    applied = applied - pen_y * (roll_rows(bottom, 1) + roll_rows(bottom, -1))
    applied = applied - pen_z * (has_prior * roll_lanes(bottom, 1) + has_next * roll_lanes(bottom, -1))
    rest = wb[0, 0] - applied
    change = element_product(0, [rest[b] for b in range(5)])
    for a in range(5):
        fin[a * 8:a * 8 + 8] = wm[0, a * 8:a * 8 + 8] + (bottom[a] + change[a])

    exchange(1, fin[0:40], fin[0:40])
    receive(1, wm, fin[0:40])
    middle_sweep(True)
    middle_sweep(False)

    def final_parts(a, c):
        u, x, y, z, slopes = window_faces(a, False)[0]
        for d in range(3):
            wsl[0, d, a] = slopes[d]
        wres[0, a] = wst[0, 100] * u
        for d, terms in enumerate((x, y, z)):
            for side in range(2):
                fin[pl.ds((d * 2 + side) * 20 + a * 4, 4)] = terms[side]
        return c
    lax.fori_loop(0, 5, final_parts, 0)
    fluxes(1)

    def both(value):
        return jnp.where(low_half, value, roll_rows(value, 4))

    low_a, low_b = halves(1.0, NEAR), halves(0.0, FAR)
    high_a, high_b = halves(FAR, 0.0), halves(NEAR, 1.0)

    def spread_z(v0, v1):
        return low_a * v0 + low_b * v1, high_a * v0 + high_b * v1

    def spread_line(v0, v1):
        return v0, NEAR * v0 + FAR * v1, FAR * v0 + NEAR * v1, v1

    def prolong(value):
        value = both(value)
        z0, z1 = spread_z(value[:, :, 0], value[:, :, 1])
        pairs = jnp.stack([z0, z1], axis=2)
        lines = jnp.concatenate([v for v in spread_line(pairs[:, 0], pairs[:, 1])], axis=1)
        return spread_line(lines[0], lines[1])

    def final_fine(a, c):
        for i, value in enumerate(prolong(wm[0, pl.ds(a * 8, 8)].reshape(2, 2, 2, 8, 128))):
            x_ref[a, i] = x_ref[a, i] + value
        volume = wres[0, a].reshape(2, 2, 2, 8, 128) + wc[0, 0, a].reshape(1, 2, 2, 8, 128)
        volume = volume + wc[0, 1, a].reshape(2, 1, 2, 8, 128) + wc[0, 2, a].reshape(2, 2, 1, 8, 128)
        for i, value in enumerate(prolong(volume)):
            res[a, i] = res[a, i] - value
        for side in range(2):
            i, j, k2 = 3 * side, slice(6 * side, 6 * side + 2), side
            face = both(fin[pl.ds(side * 20 + a * 4, 4)].reshape(2, 2, 8, 128))
            z = jnp.stack(spread_z(face[:, 0], face[:, 1]), axis=1)
            res[a, i] = res[a, i] - jnp.concatenate(spread_line(z[0], z[1]), axis=0)
            face = both(fin[pl.ds((2 + side) * 20 + a * 4, 4)].reshape(2, 2, 8, 128))
            z = jnp.stack(spread_z(face[:, 0], face[:, 1]), axis=1)
            for m, value in enumerate(spread_line(z[0], z[1])):
                res[a, m, j] = res[a, m, j] - value
            face = fin[pl.ds((4 + side) * 20 + a * 4, 4)].reshape(2, 2, 8, 128)
            face = lower * face if side == 0 else upper * roll_rows(face, 4)
            lines = jnp.stack(spread_line(face[:, 0], face[:, 1]), axis=1)
            for m, value in enumerate(spread_line(lines[0], lines[1])):
                for n in range(4):
                    res[a, m, 2 * n + k2] = res[a, m, 2 * n + k2] - value[n]
        return c
    lax.fori_loop(0, 5, final_fine, 0)
    smooth(res, False)

    send_faces(2)
    residual()
    add_halo(2)
    smooth(res, False)

    for stage in range(3):
        for direction in range(4):
            sent(*fine_message(stage, direction))
    for direction in range(8):
        sent(*static_message(direction))
    for stage in range(2):
        for direction in range(8):
            sent(*coarse_message(stage, direction))


def solution(mesh):
    sec_count, dom_count = mesh.shape["sec"], mesh.shape["dom"]

    def on_device(defect, point_inverse, flux_jacobian, time_term, penalty, element_inverse):
        def run(*refs):
            kernel(sec_count, dom_count, *refs)

        vmem = lambda *shape: pltpu.VMEM(shape + (8, 128), F32)
        dma = lambda *shape: pltpu.SemaphoreType.DMA(shape)
        out = pl.pallas_call(
            run,
            out_shape=jax.ShapeDtypeStruct((5, 4, 8, 8, 128), F32),
            in_specs=[pl.BlockSpec(memory_space=pltpu.VMEM)] * 6,
            out_specs=pl.BlockSpec(memory_space=pltpu.VMEM),
            scratch_shapes=[
                vmem(100), vmem(104), vmem(2, 8), vmem(5, 4, 8), vmem(5, 4, 8), vmem(5, 4, 8),
                vmem(3, 4, 5, 2), vmem(3, 4, 5, 2), vmem(4, 26), vmem(4, 26),
                vmem(2, 4, 15), vmem(2, 4, 15), vmem(2, 4, 5), vmem(2, 4, 5), vmem(4, 13), vmem(4, 13),
                vmem(2, 104), vmem(2, 40), vmem(2, 40), vmem(2, 5, 8), vmem(2, 3, 5, 4), vmem(2, 3, 5, 4),
                vmem(20), vmem(20), vmem(2, 2, 5), vmem(120),
                dma(3, 4), dma(3, 4), dma(8), dma(8), dma(2, 8), dma(2, 8),
            ],
            compiler_params=pltpu.CompilerParams(
                collective_id=0, has_side_effects=True, vmem_limit_bytes=48 << 20
            ),
        )(
            defect.reshape(5, 4, 8, 8, 128),
            point_inverse.reshape(5, 5, 4, 8, 8, 128),
            flux_jacobian.reshape(75, 4, 128),
            time_term,
            penalty,
            element_inverse.reshape(25, 4, 128),
        )
        return out.reshape(5, 64, 4, 128)

    placed = (
        P(None, None, "sec", "dom"),
        P(None, None, None, "sec", "dom"),
        P(None, None, None, "sec", "dom"),
        P("sec", "dom"),
        P(None, "sec", "dom"),
        P(None, None, "sec", "dom"),
    )
    return jax.shard_map(
        on_device,
        mesh=mesh,
        in_specs=placed,
        out_specs=P(None, None, "sec", "dom"),
        check_vma=False,
    )
```

profile of v0, /device:TPU:6, one launch (start us, length us, event | category | flops | bytes accessed | tf_op | source)
XLA Modules:
  0.0 43.8 jit_solution(4622052273208887695)
XLA Ops:
  0.0 0.0 copy-start
  0.0 1.9 %copy-done = f32[5,5,64,4,128]{4,3,2,1,0:T(4,128)S(1)} copy-done((f32[5,5,64,4,128]{4,3,2,1,0:T(4,128)S(1)}, f32[5,5,64,4,128]{4,3,2,1,0:T(4,128)}, u32[]{:S(2)}) %copy-start) | copy-done | bytes 3276824
  1.9 0.0 copy-start.1
  1.9 1.1 %copy-done.1 = f32[5,64,4,128]{3,2,1,0:T(4,128)S(1)} copy-done((f32[5,64,4,128]{3,2,1,0:T(4,128)S(1)}, f32[5,64,4,128]{3,2,1,0:T(4,128)}, u32[]{:S(2)}) %copy-start.1) | copy-done | bytes 655384
  3.0 0.0 copy-start.2
  3.0 0.9 %copy-done.2 = f32[3,5,5,4,128]{4,3,2,1,0:T(4,128)S(1)} copy-done((f32[3,5,5,4,128]{4,3,2,1,0:T(4,128)S(1)}, f32[3,5,5,4,128]{4,3,2,1,0:T(4,128)}, u32[]{:S(2)}) %copy-start.2) | copy-done | bytes 153624
  3.9 0.0 copy-start.3
  3.9 0.8 %copy-done.3 = f32[5,5,4,128]{3,2,1,0:T(4,128)S(1)} copy-done((f32[5,5,4,128]{3,2,1,0:T(4,128)S(1)}, f32[5,5,4,128]{3,2,1,0:T(4,128)}, u32[]{:S(2)}) %copy-start.3) | copy-done | bytes 51224
  4.7 0.0 copy-start.4
  4.7 0.7 %copy-done.4 = f32[3,4,128]{2,1,0:T(4,128)S(1)} copy-done((f32[3,4,128]{2,1,0:T(4,128)S(1)}, f32[3,4,128]{2,1,0:T(4,128)}, u32[]{:S(2)}) %copy-start.4) | copy-done | bytes 6168
  5.4 0.0 copy-start.5
  5.4 0.7 %copy-done.5 = f32[4,128]{1,0:T(4,128)S(1)} copy-done((f32[4,128]{1,0:T(4,128)S(1)}, f32[4,128]{1,0:T(4,128)}, u32[]{:S(2)}) %copy-start.5) | copy-done | bytes 2072
  6.1 36.9 %shard_map.64 = f32[5,4,8,8,128]{4,3,2,1,0:T(8,128)S(1)} custom-call(f32[5,4,8,8,128]{4,3,2,1,0:T(8,128)S(1)} %bitcast.7, f32[5,5,4,8,8,128]{5,4,3,2,1,0:T(8,128)S(1)} %bitcast.5, f32[75,4,128]{2,1,0:T(4,128)S(1)} %bitcast.8, f32[4,128]{1,0:T(4,128)S(1)} %copy-done.5, f32[3,4,128]{2,1,0:T(4,128)S(1)} %copy-done.4, f32[25,4,128]{2,1,0:T(4,128)S(1)} %bitcast.9), custom_call_target="tpu_custom_call" | custom-call | tf_op jit(solution)/shard_map/pallas_call | solution.py:657
  43.0 0.8 %copy.8 = f32[5,64,4,128]{3,2,1,0:T(4,128)} copy(f32[5,64,4,128]{3,2,1,0:T(4,128)S(1)} %bitcast.6) | data formatting | bytes 1310720
Async XLA Ops:
  0.0 1.9 %copy-start = (f32[5,5,64,4,128]{4,3,2,1,0:T(4,128)S(1)}, f32[5,5,64,4,128]{4,3,2,1,0:T(4,128)}, u32[]{:S(2)}) copy-start(f32[5,5,64,4,128]{4,3,2,1,0:T(4,128)} %param.7) | copy-start | bytes 9830404
  1.9 1.1 %copy-start.1 = (f32[5,64,4,128]{3,2,1,0:T(4,128)S(1)}, f32[5,64,4,128]{3,2,1,0:T(4,128)}, u32[]{:S(2)}) copy-start(f32[5,64,4,128]{3,2,1,0:T(4,128)} %param.6) | copy-start | bytes 1966084
  3.0 0.9 %copy-start.2 = (f32[3,5,5,4,128]{4,3,2,1,0:T(4,128)S(1)}, f32[3,5,5,4,128]{4,3,2,1,0:T(4,128)}, u32[]{:S(2)}) copy-start(f32[3,5,5,4,128]{4,3,2,1,0:T(4,128)} %param.8) | copy-start | bytes 460804
  3.9 0.8 %copy-start.3 = (f32[5,5,4,128]{3,2,1,0:T(4,128)S(1)}, f32[5,5,4,128]{3,2,1,0:T(4,128)}, u32[]{:S(2)}) copy-start(f32[5,5,4,128]{3,2,1,0:T(4,128)} %param.11) | copy-start | bytes 153604
  4.7 0.7 %copy-start.4 = (f32[3,4,128]{2,1,0:T(4,128)S(1)}, f32[3,4,128]{2,1,0:T(4,128)}, u32[]{:S(2)}) copy-start(f32[3,4,128]{2,1,0:T(4,128)} %refs_4_.1) | copy-start | bytes 18436
  5.4 0.7 %copy-start.5 = (f32[4,128]{1,0:T(4,128)S(1)}, f32[4,128]{1,0:T(4,128)}, u32[]{:S(2)}) copy-start(f32[4,128]{1,0:T(4,128)} %refs_3_.1) | copy-start | bytes 6148
where the time goes:
time: 44.1 us; the launch traced here: 43.8 us
  Pallas kernels  36.9 us (84%)
  local copies, waits for them, and re-layouts  6.94 us (16%)
    pallas_call x1, Pallas kernels, on_device(): pl.pallas_call(run, out_shape=jax.ShapeDtypeStruct((5, 4, 8, 8, 128), F32...  36.9 us
    unnamed x13, local copies, waits for them, and re-layouts  6.94 us

commit v1 on v0

--- a/solution.py
+++ b/solution.py
@@ -45,24 +45,26 @@
     return value if shift == 0 else pltpu.roll(value, shift, value.ndim - 2)
 
 
-def line_slopes(u0, u1, u2, u3):
-    outer, inner = u0 - u3, u1 - u2
-    even = (u0 + u3) - (u1 + u2)
-    e0, e1 = EVEN[0] * even, EVEN[1] * even
-    o0 = ODD[0][0] * outer + ODD[0][1] * inner
-    o1 = ODD[1][0] * outer + ODD[1][1] * inner
-    return o0 + e0, o1 + e1, o1 - e1, o0 - e0
-
-
 def kernel(
     sec_count, dom_count,
+    s_hbm, b_hbm, j_hbm, t_hbm, p_hbm, e_hbm,
+    out_ref,
     s_ref, b_ref, j_ref, t_ref, p_ref, e_ref,
-    x_ref,
-    jd, own, dg, res, sly, slz,
+    x_ref, jd, own, dg, res,
     fsend, frecv, ssend, srecv, esend, erecv, dsend, drecv, dssend, dsrecv,
     wst, wm, ws, wres, wsl, wc, wrx, wry, wb, fin,
-    f_ss, f_rs, s_ss, s_rs, e_ss, e_rs,
+    f_ss, f_rs, s_ss, s_rs, e_ss, e_rs, in_sem,
 ):
+    small = [
+        pltpu.make_async_copy(source, kept, in_sem.at[4 + n])
+        for n, (source, kept) in enumerate(
+            ((s_hbm, s_ref), (j_hbm, j_ref), (e_hbm, e_ref), (t_hbm, t_ref), (p_hbm, p_ref)))
+    ]
+    blocks = [
+        pltpu.make_async_copy(b_hbm.at[:, :, i], b_ref.at[:, :, i], in_sem.at[i]) for i in range(4)
+    ]
+    for transfer in small + blocks:
+        transfer.start()
     me_sec, me_dom = lax.axis_index("sec"), lax.axis_index("dom")
     has_dom = {0: None, 1: me_dom < dom_count - 1, -1: me_dom > 0}
     has_sec = {0: None, 1: me_sec < sec_count - 1, -1: me_sec > 0}
@@ -149,25 +151,25 @@
     def halves(a, b):
         return jnp.where(low_half, F32(a), F32(b))
 
+    for transfer in small[1:]:
+        transfer.wait()
     for array, start, count, scale in ((j_ref, 0, 75, 0.5), (e_ref, 75, 25, DAMPING)):
-        def spread(n, c, array=array, start=start, scale=scale):
-            value = array[n]
-            jd[start + n, 0:4] = value
-            jd[start + n, 4:8] = value
-            own[start + n] = scale * jd[start + n]
-            return c
-        lax.fori_loop(0, count, spread, 0)
+        value = array[...]
+        jd[start:start + count, 0:4] = value
+        jd[start:start + count, 4:8] = value
+    own[0:75] = 0.5 * jd[0:75]
+    own[75:100] = DAMPING * jd[75:100]
     for n, value in enumerate((t_ref[...], p_ref[0], p_ref[1], p_ref[2])):
         own[100 + n, 0:4] = value
         own[100 + n, 4:8] = value
     time, pen_x, pen_y, pen_z = own[100], own[101], own[102], own[103]
     for f in range(2):
-        for q in range(8):
-            j, k2 = q // 2, q % 2
-            total = time + pen_z * (lower if k2 == 0 else upper)
-            if j in (0, 3):
-                total = total + pen_y
-            dg[f, q] = total + pen_x if f else total
+        for j in range(4):
+            for k2 in range(2):
+                total = time + pen_z * (lower if k2 == 0 else upper)
+                if j in (0, 3):
+                    total = total + pen_y
+                dg[f, j, k2] = total + pen_x if f else total
 
     px_prior = jnp.where(lane >= EZ, pen_x, 0.0)
     px_next = jnp.where(lane < 128 - EZ, pen_x, 0.0)
@@ -181,15 +183,22 @@
     pz_prior = pen_z * lower * has_prior
     pz_next = pen_z * upper * has_next
 
-    def smooth(source, first):
-        def block(q, c):
-            values = [source[a, :, q] for a in range(5)]
-            for a in range(5):
-                total = b_ref[a, 0, :, q] * values[0]
-                for b in range(1, 5):
-                    total = total + b_ref[a, b, :, q] * values[b]
-                total = DAMPING * total
-                x_ref[a, :, q] = total if first else x_ref[a, :, q] + total
+    def smooth(source, i, j, target, first):
+        part = pl.ds(j, 2)
+        values = [source[a, i, part] for a in range(5)]
+        totals = []
+        for a in range(5):
+            total = b_ref[a, 0, i, part] * values[0]
+            for b in range(1, 5):
+                total = total + b_ref[a, b, i, part] * values[b]
+            total = DAMPING * total
+            totals.append(total if first else x_ref[a, i, part] + total)
+        for a in range(5):
+            target[a, i, part] = totals[a]
+
+    def smooth_all(target):
+        def block(n, c):
+            smooth(res, n // 2, 2 * (n % 2), target, False)
             return c
         lax.fori_loop(0, 8, block, 0)
 
@@ -201,90 +210,130 @@
                 packed = piece if packed is None else jnp.where(place == m, piece, packed)
             return packed
 
-        def one_variable(a, c):
-            fsend[stage, RIGHT, a] = pieces(
-                lambda m: x_ref[a, 3, 2 * m:2 * m + 2], lambda v, m: roll_lanes(v, EZ * (m + 1)), lane // EZ)
-            fsend[stage, LEFT, a] = pieces(
-                lambda m: x_ref[a, 0, 2 * m:2 * m + 2], lambda v, m: roll_lanes(v, EZ * m), lane // EZ)
-            fsend[stage, UP, a] = pieces(
-                lambda m: x_ref[a, m, 6:8], lambda v, m: roll_rows(v, m - 3), row4)
-            fsend[stage, DOWN, a] = pieces(
-                lambda m: x_ref[a, m, 0:2], lambda v, m: roll_rows(v, m), row4)
-            return c
-        lax.fori_loop(0, 5, one_variable, 0)
-        for direction in range(4):
+        fsend[stage, RIGHT] = pieces(
+            lambda m: x_ref[:, 3, m], lambda v, m: roll_lanes(v, EZ * (m + 1)), lane // EZ)
+        fsend[stage, LEFT] = pieces(
+            lambda m: x_ref[:, 0, m], lambda v, m: roll_lanes(v, EZ * m), lane // EZ)
+        for direction in (RIGHT, LEFT):
             send(*fine_message(stage, direction))
-
-    even_z = halves(EVEN[0], -EVEN[1])
-    even_z_swapped = halves(EVEN[1], -EVEN[0])
+        fsend[stage, UP] = pieces(
+            lambda m: x_ref[:, m, 3], lambda v, m: roll_rows(v, m - 3), row4)
+        fsend[stage, DOWN] = pieces(
+            lambda m: x_ref[:, m, 0], lambda v, m: roll_rows(v, m), row4)
+        for direction in (UP, DOWN):
+            send(*fine_message(stage, direction))
+
+    even_z = halves(EVEN[0], EVEN[1])
+    even_z_swapped = halves(EVEN[1], EVEN[0])
     odd_z = halves(ODD[0][0], ODD[1][1])
     odd_z_cross = halves(ODD[0][1], ODD[1][0])
     odd_z_swapped = halves(ODD[1][1], ODD[0][0])
     odd_z_cross_swapped = halves(ODD[1][0], ODD[0][1])
 
+    def jacobian(d, parts):
+        out = []
+        for a in range(5):
+            total = [jd[d * 25 + a * 5] * value for value in parts[0]]
+            for b in range(1, 5):
+                block = jd[d * 25 + a * 5 + b]
+                total = [t + block * value for t, value in zip(total, parts[b])]
+            out.append(total)
+        return out
+
+    def line_parts(u):
+        return [u[0] - u[3], u[1] - u[2], (u[0] + u[3]) - (u[1] + u[2])]
+
+    def line_slopes(outer, inner, even):
+        e0, e1 = EVEN[0] * even, EVEN[1] * even
+        o0 = ODD[0][0] * outer + ODD[0][1] * inner
+        o1 = ODD[1][0] * outer + ODD[1][1] * inner
+        return o0 + e0, o1 + e1, o1 - e1, o0 - e0
+
     def residual():
-        def slab(n, c):
-            a, i = n // 4, n % 4
-            face = 1 - ((i + 1) // 2) % 2
-            u = x_ref[a, i]
-            r = s_ref[a, i] - dg[face] * u
-            pairs = u.reshape(4, 2, 8, 128)
-            v0, v1 = pairs[:, 0], pairs[:, 1]
-            w0, w1 = roll_rows(v0, 4), roll_rows(v1, 4)
-            even = (v0 + w1) - (w0 + v1)
-            outer, inner = v0 - w1, w0 - v1
-            z0 = odd_z * outer + odd_z_cross * inner + even_z * even
-            z1 = odd_z_swapped * inner + odd_z_cross_swapped * outer - even_z_swapped * even
-            slz[a, i] = jnp.stack([z0, z1], axis=1).reshape(8, 8, 128)
-            add0 = pz_prior * roll_lanes(w1, 1)
-            add1 = pz_next * roll_lanes(w0, -1)
-            r = r + jnp.stack([add0, add1], axis=1).reshape(8, 8, 128)
-            y = line_slopes(u[0:2], u[2:4], u[4:6], u[6:8])
-            sly[a, i] = jnp.concatenate(y, axis=0)
-            first = r[0:2] + py_prior * roll_rows(u[6:8], 1)
-            last = r[6:8] + py_next * roll_rows(u[0:2], -1)
-            res[a, i] = jnp.concatenate([first, r[2:6], last], axis=0)
+        def along_x(n, c):
+            j, k2 = n // 2, n % 2
+            inner_weight, outer_weight = dg[0, j, k2], dg[1, j, k2]
+            u = [x_ref[a, :, j, k2] for a in range(5)]
+            flux = jacobian(0, [line_parts(v) for v in u])
+            out = []
+            for a in range(5):
+                slopes = line_slopes(*flux[a])
+                s = s_ref[a, :, j, k2]
+                v = u[a]
+                out.append(jnp.stack([
+                    (s[0] - outer_weight * v[0]) + (px_prior * roll_lanes(v[3], EZ) - slopes[0]),
+                    (s[1] - inner_weight * v[1]) - slopes[1],
+                    (s[2] - inner_weight * v[2]) - slopes[2],
+                    (s[3] - outer_weight * v[3]) + (px_next * roll_lanes(v[0], -EZ) - slopes[3]),
+                ]))
+            for a in range(5):
+                res[a, :, j, k2] = out[a]
             return c
-        lax.fori_loop(0, 20, slab, 0)
-
-        def block(q, c):
-            total, slopes = [], []
-            for a in range(5):
-                u = x_ref[a, :, q]
-                r = res[a, :, q]
-                first = r[0] + px_prior * roll_lanes(u[3], EZ)
-                last = r[3] + px_next * roll_lanes(u[0], -EZ)
-                total.append(jnp.stack([first, r[1], r[2], last]))
-                slopes.append(jnp.stack(line_slopes(u[0], u[1], u[2], u[3])))
-            for d in range(3):
-                if d == 1:
-                    slopes = [sly[a, :, q] for a in range(5)]
-                if d == 2:
-                    slopes = [slz[a, :, q] for a in range(5)]
-                for a in range(5):
-                    for b in range(5):
-                        total[a] = total[a] - jd[d * 25 + a * 5 + b] * slopes[b]
-            for a in range(5):
-                res[a, :, q] = total[a]
+        lax.fori_loop(0, 8, along_x, 0)
+
+        def along_y(n, c):
+            i, k2 = n // 2, n % 2
+            u = [x_ref[a, i, :, k2] for a in range(5)]
+            flux = jacobian(1, [line_parts(v) for v in u])
+            out = []
+            for a in range(5):
+                slopes = line_slopes(*flux[a])
+                r = res[a, i, :, k2]
+                v = u[a]
+                out.append(jnp.stack([
+                    r[0] + (py_prior * roll_rows(v[3], 1) - slopes[0]),
+                    r[1] - slopes[1],
+                    r[2] - slopes[2],
+                    r[3] + (py_next * roll_rows(v[0], -1) - slopes[3]),
+                ]))
+            for a in range(5):
+                res[a, i, :, k2] = out[a]
             return c
-        lax.fori_loop(0, 8, block, 0)
+        lax.fori_loop(0, 8, along_y, 0)
+
+        def along_z(n, c):
+            i, j = n // 2, 2 * (n % 2)
+            part = pl.ds(j, 2)
+            parts, adds = [], []
+            for a in range(5):
+                u = x_ref[a, i, part]
+                v0, v1 = u[:, 0], u[:, 1]
+                w0, w1 = roll_rows(v0, 4), roll_rows(v1, 4)
+                straight, swapped = v0 + w1, w0 + v1
+                odd = v0 - w1
+                even = jnp.where(low_half, straight[0] - swapped[0], swapped[1] - straight[1])
+                parts.append([odd[0], odd[1], even])
+                adds.append(jnp.stack([pz_prior * roll_lanes(w1, 1), pz_next * roll_lanes(w0, -1)], axis=1))
+            flux = jacobian(2, parts)
+            out = []
+            for a in range(5):
+                turned = roll_rows(flux[a][2], 4)
+                even = (jnp.where(low_half, flux[a][2], turned), jnp.where(low_half, turned, flux[a][2]))
+                lines = []
+                for m in range(2):
+                    odd = flux[a][m]
+                    cross = roll_rows(odd, 4)
+                    lines.append(jnp.stack([
+                        odd_z * odd + odd_z_cross * cross + even_z * even[m],
+                        odd_z_swapped * cross + odd_z_cross_swapped * odd - even_z_swapped * even[m],
+                    ]))
+                out.append(res[a, i, part] + (adds[a] - jnp.stack(lines)))
+            for a in range(5):
+                res[a, i, part] = out[a]
+            return c
+        lax.fori_loop(0, 8, along_z, 0)
 
     def add_halo(stage):
         for direction in range(4):
             arrived(*fine_message(stage, direction))
-
-        def one_variable(a, c):
-            from_left, from_right = frecv[stage, RIGHT, a], frecv[stage, LEFT, a]
-            from_below, from_above = frecv[stage, UP, a], frecv[stage, DOWN, a]
-            for m in range(4):
-                q = slice(2 * m, 2 * m + 2)
-                res[a, 0, q] = res[a, 0, q] + px_left * roll_lanes(from_left, -EZ * m)
-                res[a, 3, q] = res[a, 3, q] + px_right * roll_lanes(from_right, 128 - EZ * (m + 1))
-            for m in range(4):
-                res[a, m, 0:2] = res[a, m, 0:2] + py_below * roll_rows(from_below, -m)
-                res[a, m, 6:8] = res[a, m, 6:8] + py_above * roll_rows(from_above, 3 - m)
-            return c
-        lax.fori_loop(0, 5, one_variable, 0)
+        from_left, from_right = frecv[stage, RIGHT], frecv[stage, LEFT]
+        from_below, from_above = frecv[stage, UP], frecv[stage, DOWN]
+        for m in range(4):
+            res[:, 0, m] = res[:, 0, m] + px_left * roll_lanes(from_left, -EZ * m)
+            res[:, 3, m] = res[:, 3, m] + px_right * roll_lanes(from_right, 128 - EZ * (m + 1))
+        for m in range(4):
+            res[:, m, 0] = res[:, m, 0] + py_below * roll_rows(from_below, -m)
+            res[:, m, 3] = res[:, m, 3] + py_above * roll_rows(from_above, 3 - m)
 
     def pack_columns(value, first_block):
         quarter = value.shape[0] // 4
@@ -333,7 +382,11 @@
             window[0, part] = jnp.where(low_half, mine[part], ends[m])
             window[1, part] = jnp.where(low_half, side[m], edge[m])
 
-    smooth(s_ref, True)
+    small[0].wait()
+    for i in range(4):
+        blocks[i].wait()
+        for j in (0, 2):
+            smooth(s_ref, i, j, x_ref, True)
     pl.semaphore_wait(barrier, across * along - 1)
     send_faces(0)
 
@@ -363,9 +416,13 @@
 
     residual()
     add_halo(0)
-    smooth(res, False)
+    smooth_all(x_ref)
     send_faces(1)
     residual()
+    for direction in range(4):
+        sent(*fine_message(0, direction))
+    for direction in range(8):
+        sent(*static_message(direction))
     for direction in range(8):
         arrived(*static_message(direction))
     fill_window(
@@ -378,7 +435,7 @@
     near_low, far_low = halves(1.0, NEAR), halves(FAR, 0.0)
     near_high, far_high = halves(NEAR, 1.0), halves(0.0, FAR)
 
-    def restrict(a, c):
+    for a in range(5):
         for ip in range(2):
             if ip == 0:
                 x = res[a, 0] + NEAR * res[a, 1] + FAR * res[a, 2]
@@ -386,16 +443,14 @@
                 x = FAR * res[a, 1] + NEAR * res[a, 2] + res[a, 3]
             for jp in range(2):
                 if jp == 0:
-                    y = x[0:2] + NEAR * x[2:4] + FAR * x[4:6]
+                    y = x[0] + NEAR * x[1] + FAR * x[2]
                 else:
-                    y = FAR * x[2:4] + NEAR * x[4:6] + x[6:8]
+                    y = FAR * x[1] + NEAR * x[2] + x[3]
                 z0 = near_low * y[0] + far_low * y[1]
                 z1 = far_high * y[0] + near_high * y[1]
                 n = a * 8 + ip * 4 + jp * 2
                 fin[n] = z0 + roll_rows(z0, 4)
                 fin[n + 1] = z1 + roll_rows(z1, 4)
-        return c
-    lax.fori_loop(0, 5, restrict, 0)
 
     def exchange(stage, field, faces):
         nodes = faces.reshape(5, 2, 2, 2, 8, 128)
@@ -474,23 +529,29 @@
         def one(n, c):
             d, tile = n // tiles, n % tiles
             slopes = [wsl[tile, d, b] for b in range(5)]
+            totals = []
             for a in range(5):
                 total = wst[tile, d * 25 + a * 5] * slopes[0]
                 for b in range(1, 5):
                     total = total + wst[tile, d * 25 + a * 5 + b] * slopes[b]
-                wc[tile, d, a] = total
+                totals.append(total)
+            for a in range(5):
+                wc[tile, d, a] = totals[a]
             return c
         lax.fori_loop(0, 3 * tiles, one, 0)
 
     def middle_residual(use_strips):
         def one(a, c):
+            rest = []
             for tile, (u, x, y, z, slopes) in enumerate(window_faces(a, use_strips)):
                 r = ws[tile, pl.ds(a * 8, 8)] - wst[tile, 100] * u
                 r = r.reshape(2, 2, 2, 8, 128)
                 r = r - jnp.stack(x, axis=0).reshape(2, 2, 2, 8, 128)
                 r = r - jnp.stack([v.reshape(2, 2, 8, 128) for v in y], axis=1)
                 r = r - jnp.stack([v.reshape(2, 2, 8, 128) for v in z], axis=2)
-                wres[tile, a] = r.reshape(8, 8, 128)
+                rest.append((r.reshape(8, 8, 128), slopes))
+            for tile, (r, slopes) in enumerate(rest):
+                wres[tile, a] = r
                 for d in range(3):
                     wsl[tile, d, a] = slopes[d]
             return c
@@ -502,21 +563,6 @@
         r = r - wc[tile, 0, a].reshape(2, 2, 8, 128)
         r = r - wc[tile, 1, a, pl.ds(ip * 2, 2)][None]
         return r - wc[tile, 2, a, pl.ds(ip * 2, 2)][:, None]
-
-    def middle_sweep(use_strips):
-        middle_residual(use_strips)
-
-        def one(n, c):
-            tile, ip = n // 2, n % 2
-            r = [full_residual(tile, ip, a).reshape(4, 8, 128) for a in range(5)]
-            for a in range(5):
-                part = pl.ds(a * 8 + ip * 4, 4)
-                total = wm[tile, part]
-                for b in range(5):
-                    total = total + wst[tile, 75 + a * 5 + b] * r[b]
-                wm[tile, part] = total
-            return c
-        lax.fori_loop(0, 4, one, 0)
 
     def element_product(tile, values):
         out = []
@@ -526,6 +572,19 @@
                 total = total + wst[tile, 75 + a * 5 + b] * values[b]
             out.append(total)
         return out
+
+    def middle_sweep(use_strips):
+        middle_residual(use_strips)
+
+        def one(n, c):
+            tile, ip = n // 2, n % 2
+            r = [full_residual(tile, ip, a).reshape(4, 8, 128) for a in range(5)]
+            parts = [pl.ds(a * 8 + ip * 4, 4) for a in range(5)]
+            totals = [wm[tile, part] + change for part, change in zip(parts, element_product(tile, r))]
+            for part, total in zip(parts, totals):
+                wm[tile, part] = total
+            return c
+        lax.fori_loop(0, 4, one, 0)
 
     def own_guess(n, c):
         part = [fin[pl.ds(b * 8 + n * 4, 4)] for b in range(5)]
@@ -601,48 +660,55 @@
         value = both(value)
         z0, z1 = spread_z(value[:, :, 0], value[:, :, 1])
         pairs = jnp.stack([z0, z1], axis=2)
-        lines = jnp.concatenate([v for v in spread_line(pairs[:, 0], pairs[:, 1])], axis=1)
+        lines = jnp.stack(spread_line(pairs[:, 0], pairs[:, 1]), axis=1)
         return spread_line(lines[0], lines[1])
 
     def final_fine(a, c):
-        for i, value in enumerate(prolong(wm[0, pl.ds(a * 8, 8)].reshape(2, 2, 2, 8, 128))):
-            x_ref[a, i] = x_ref[a, i] + value
+        guess = [x_ref[a, i] + value
+                 for i, value in enumerate(prolong(wm[0, pl.ds(a * 8, 8)].reshape(2, 2, 2, 8, 128)))]
         volume = wres[0, a].reshape(2, 2, 2, 8, 128) + wc[0, 0, a].reshape(1, 2, 2, 8, 128)
         volume = volume + wc[0, 1, a].reshape(2, 1, 2, 8, 128) + wc[0, 2, a].reshape(2, 2, 1, 8, 128)
-        for i, value in enumerate(prolong(volume)):
-            res[a, i] = res[a, i] - value
+        rest = [[[res[a, i, j, k2] - value[j, k2] for k2 in range(2)] for j in range(4)]
+                for i, value in enumerate(prolong(volume))]
         for side in range(2):
-            i, j, k2 = 3 * side, slice(6 * side, 6 * side + 2), side
+            end = 3 * side
             face = both(fin[pl.ds(side * 20 + a * 4, 4)].reshape(2, 2, 8, 128))
             z = jnp.stack(spread_z(face[:, 0], face[:, 1]), axis=1)
-            res[a, i] = res[a, i] - jnp.concatenate(spread_line(z[0], z[1]), axis=0)
+            for m, value in enumerate(spread_line(z[0], z[1])):
+                for k2 in range(2):
+                    rest[end][m][k2] = rest[end][m][k2] - value[k2]
             face = both(fin[pl.ds((2 + side) * 20 + a * 4, 4)].reshape(2, 2, 8, 128))
             z = jnp.stack(spread_z(face[:, 0], face[:, 1]), axis=1)
             for m, value in enumerate(spread_line(z[0], z[1])):
-                res[a, m, j] = res[a, m, j] - value
+                for k2 in range(2):
+                    rest[m][end][k2] = rest[m][end][k2] - value[k2]
             face = fin[pl.ds((4 + side) * 20 + a * 4, 4)].reshape(2, 2, 8, 128)
             face = lower * face if side == 0 else upper * roll_rows(face, 4)
             lines = jnp.stack(spread_line(face[:, 0], face[:, 1]), axis=1)
             for m, value in enumerate(spread_line(lines[0], lines[1])):
                 for n in range(4):
-                    res[a, m, 2 * n + k2] = res[a, m, 2 * n + k2] - value[n]
+                    rest[m][n][side] = rest[m][n][side] - value[n]
+        for i in range(4):
+            x_ref[a, i] = guess[i]
+            for j in range(4):
+                for k2 in range(2):
+                    res[a, i, j, k2] = rest[i][j][k2]
         return c
     lax.fori_loop(0, 5, final_fine, 0)
-    smooth(res, False)
+    smooth_all(x_ref)
 
     send_faces(2)
     residual()
-    add_halo(2)
-    smooth(res, False)
-
-    for stage in range(3):
-        for direction in range(4):
-            sent(*fine_message(stage, direction))
-    for direction in range(8):
-        sent(*static_message(direction))
     for stage in range(2):
         for direction in range(8):
             sent(*coarse_message(stage, direction))
+    for direction in range(4):
+        sent(*fine_message(1, direction))
+    add_halo(2)
+    smooth_all(out_ref)
+
+    for direction in range(4):
+        sent(*fine_message(2, direction))
 
 
 def solution(mesh):
@@ -656,27 +722,34 @@
         dma = lambda *shape: pltpu.SemaphoreType.DMA(shape)
         out = pl.pallas_call(
             run,
-            out_shape=jax.ShapeDtypeStruct((5, 4, 8, 8, 128), F32),
-            in_specs=[pl.BlockSpec(memory_space=pltpu.VMEM)] * 6,
+            out_shape=jax.ShapeDtypeStruct((5, 4, 4, 2, 8, 128), F32),
+            in_specs=[pl.BlockSpec(memory_space=pltpu.HBM)] * 6,
             out_specs=pl.BlockSpec(memory_space=pltpu.VMEM),
             scratch_shapes=[
-                vmem(100), vmem(104), vmem(2, 8), vmem(5, 4, 8), vmem(5, 4, 8), vmem(5, 4, 8),
+                vmem(5, 4, 4, 2), vmem(5, 5, 4, 4, 2), pltpu.VMEM((75, 4, 128), F32), pltpu.VMEM((4, 128), F32),
+                pltpu.VMEM((3, 4, 128), F32), pltpu.VMEM((25, 4, 128), F32),
+                vmem(5, 4, 4, 2), vmem(100), vmem(104), vmem(2, 4, 2), vmem(5, 4, 4, 2),
                 vmem(3, 4, 5, 2), vmem(3, 4, 5, 2), vmem(4, 26), vmem(4, 26),
                 vmem(2, 4, 15), vmem(2, 4, 15), vmem(2, 4, 5), vmem(2, 4, 5), vmem(4, 13), vmem(4, 13),
                 vmem(2, 104), vmem(2, 40), vmem(2, 40), vmem(2, 5, 8), vmem(2, 3, 5, 4), vmem(2, 3, 5, 4),
                 vmem(20), vmem(20), vmem(2, 2, 5), vmem(120),
-                dma(3, 4), dma(3, 4), dma(8), dma(8), dma(2, 8), dma(2, 8),
+                dma(3, 4), dma(3, 4), dma(8), dma(8), dma(2, 8), dma(2, 8), dma(9),
             ],
             compiler_params=pltpu.CompilerParams(
                 collective_id=0, has_side_effects=True, vmem_limit_bytes=48 << 20
             ),
         )(
-            defect.reshape(5, 4, 8, 8, 128),
-            point_inverse.reshape(5, 5, 4, 8, 8, 128),
-            flux_jacobian.reshape(75, 4, 128),
-            time_term,
-            penalty,
-            element_inverse.reshape(25, 4, 128),
+            *(
+                pltpu.with_memory_space_constraint(array, pltpu.HBM)
+                for array in (
+                    defect.reshape(5, 4, 4, 2, 8, 128),
+                    point_inverse.reshape(5, 5, 4, 4, 2, 8, 128),
+                    flux_jacobian.reshape(75, 4, 128),
+                    time_term,
+                    penalty,
+                    element_inverse.reshape(25, 4, 128),
+                )
+            )
         )
         return out.reshape(5, 64, 4, 128)
 

time: 44.1 us -> 35.8 us (0.81)
  local copies, waits for them, and re-layouts: 6.94 us -> 0.84 us
  Pallas kernels: 36.9 us -> 34.8 us
    unnamed x13 -> x1, local copies, waits for them, and re-layouts: 6.94 us -> 0.84 us
    pallas_call x1, Pallas kernels: 36.9 us -> 34.8 us  [on_device(): pl.pallas_call(run, out_shape=jax.ShapeDtypeStruct((5, 4, 4, 2, 8, 128),...]
where the time goes in v1:
time: 35.8 us; the launch traced here: 35.7 us
  Pallas kernels  34.8 us (97%)
  local copies, waits for them, and re-layouts  0.84 us (2%)
    pallas_call x1, Pallas kernels, on_device(): pl.pallas_call(run, out_shape=jax.ShapeDtypeStruct((5, 4, 4, 2, 8, 128),...  34.8 us
    unnamed x1, local copies, waits for them, and re-layouts  0.84 us

profile of v1, /device:TPU:6, one launch (start us, length us, event | category | flops | bytes accessed | tf_op | source)
XLA Modules:
  0.0 35.7 jit_solution(3129807247581480488)
XLA Ops:
  0.0 34.8 %shard_map.64 = f32[5,4,4,2,8,128]{5,4,3,2,1,0:T(8,128)S(1)} custom-call(f32[5,4,4,2,8,128]{5,4,3,2,1,0:T(8,128)} %bitcast.7, f32[5,5,4,4,2,8,128]{6,5,4,3,2,1,0:T(8,128)} %bitcast.6, f32[75,4,128]{2,1,0:T(4,128)} %bitcast.8, f32[4,128]{1,0:T(4,128)} %refs_3_.1, f32[3,4,128]{2,1,0:T(4,128)} %refs_4_.1, f32[25,4,128]{2,1,0:T(4,128)} %bitcast.9), custom_call_target="tpu_custom_call" | custom-call | tf_op jit(solution)/shard_map/pallas_call | solution.py:723
  34.8 0.8 %copy.8 = f32[5,64,4,128]{3,2,1,0:T(4,128)} copy(f32[5,64,4,128]{3,2,1,0:T(4,128)S(1)} %bitcast.5) | data formatting | bytes 1310720

commit v2 on v1

--- a/solution.py
+++ b/solution.py
@@ -45,6 +45,11 @@
     return value if shift == 0 else pltpu.roll(value, shift, value.ndim - 2)
 
 
+def repeat(count, body):
+    for n in range(count):
+        body(n, 0)
+
+
 def kernel(
     sec_count, dom_count,
     s_hbm, b_hbm, j_hbm, t_hbm, p_hbm, e_hbm,
@@ -52,7 +57,7 @@
     s_ref, b_ref, j_ref, t_ref, p_ref, e_ref,
     x_ref, jd, own, dg, res,
     fsend, frecv, ssend, srecv, esend, erecv, dsend, drecv, dssend, dsrecv,
-    wst, wm, ws, wres, wsl, wc, wrx, wry, wb, fin,
+    wst, wm, ws, w48, wres, wc, wrx, wry, wb, fin,
     f_ss, f_rs, s_ss, s_rs, e_ss, e_rs, in_sem,
 ):
     small = [
@@ -63,7 +68,7 @@
     blocks = [
         pltpu.make_async_copy(b_hbm.at[:, :, i], b_ref.at[:, :, i], in_sem.at[i]) for i in range(4)
     ]
-    for transfer in small + blocks:
+    for transfer in [small[0], blocks[0], blocks[3], blocks[1], blocks[2]] + small[1:]:
         transfer.start()
     me_sec, me_dom = lax.axis_index("sec"), lax.axis_index("dom")
     has_dom = {0: None, 1: me_dom < dom_count - 1, -1: me_dom > 0}
@@ -133,9 +138,11 @@
 
     def coarse_message(stage, direction):
         if direction < 4:
-            src, dst = esend.at[stage, direction], erecv.at[stage, direction]
+            part = pl.ds(0, (15, 14)[stage])
+            src, dst = esend.at[stage, direction, part], erecv.at[stage, direction, part]
         else:
-            src, dst = dsend.at[stage, direction - 4], drecv.at[stage, direction - 4]
+            part = pl.ds(0, (5, 6)[stage])
+            src, dst = dsend.at[stage, direction - 4, part], drecv.at[stage, direction - 4, part]
         return direction, src, dst, e_ss.at[stage, direction], e_rs.at[stage, direction]
 
     lane = lax.broadcasted_iota(jnp.int32, (8, 128), 1)
@@ -147,41 +154,10 @@
     has_prior = jnp.where(z_index > 0, 1.0, 0.0)
     lower = jnp.where(low_half, 1.0, 0.0)
     upper = 1.0 - lower
+    row4 = row % 4
 
     def halves(a, b):
         return jnp.where(low_half, F32(a), F32(b))
-
-    for transfer in small[1:]:
-        transfer.wait()
-    for array, start, count, scale in ((j_ref, 0, 75, 0.5), (e_ref, 75, 25, DAMPING)):
-        value = array[...]
-        jd[start:start + count, 0:4] = value
-        jd[start:start + count, 4:8] = value
-    own[0:75] = 0.5 * jd[0:75]
-    own[75:100] = DAMPING * jd[75:100]
-    for n, value in enumerate((t_ref[...], p_ref[0], p_ref[1], p_ref[2])):
-        own[100 + n, 0:4] = value
-        own[100 + n, 4:8] = value
-    time, pen_x, pen_y, pen_z = own[100], own[101], own[102], own[103]
-    for f in range(2):
-        for j in range(4):
-            for k2 in range(2):
-                total = time + pen_z * (lower if k2 == 0 else upper)
-                if j in (0, 3):
-                    total = total + pen_y
-                dg[f, j, k2] = total + pen_x if f else total
-
-    px_prior = jnp.where(lane >= EZ, pen_x, 0.0)
-    px_next = jnp.where(lane < 128 - EZ, pen_x, 0.0)
-    px_left = jnp.where(lane < EZ, pen_x, 0.0)
-    px_right = jnp.where(lane >= 128 - EZ, pen_x, 0.0)
-    row4 = row % 4
-    py_prior = jnp.where(row4 != 0, pen_y, 0.0)
-    py_next = jnp.where(row4 != 3, pen_y, 0.0)
-    py_below = jnp.where(row4 == 0, pen_y, 0.0)
-    py_above = jnp.where(row4 == 3, pen_y, 0.0)
-    pz_prior = pen_z * lower * has_prior
-    pz_next = pen_z * upper * has_next
 
     def smooth(source, i, j, target, first):
         part = pl.ds(j, 2)
@@ -196,26 +172,26 @@
         for a in range(5):
             target[a, i, part] = totals[a]
 
-    def smooth_all(target):
-        def block(n, c):
-            smooth(res, n // 2, 2 * (n % 2), target, False)
-            return c
-        lax.fori_loop(0, 8, block, 0)
-
-    def send_faces(stage):
-        def pieces(face, rolled, place):
-            packed = None
-            for m in range(4):
-                piece = rolled(face(m), m)
-                packed = piece if packed is None else jnp.where(place == m, piece, packed)
-            return packed
-
+    def smooth_slab(source, i, target, first=False):
+        for j in (0, 2):
+            smooth(source, i, j, target, first)
+
+    def pieces(face, rolled, place):
+        packed = None
+        for m in range(4):
+            piece = rolled(face(m), m)
+            packed = piece if packed is None else jnp.where(place == m, piece, packed)
+        return packed
+
+    def send_x_faces(stage):
         fsend[stage, RIGHT] = pieces(
             lambda m: x_ref[:, 3, m], lambda v, m: roll_lanes(v, EZ * (m + 1)), lane // EZ)
         fsend[stage, LEFT] = pieces(
             lambda m: x_ref[:, 0, m], lambda v, m: roll_lanes(v, EZ * m), lane // EZ)
         for direction in (RIGHT, LEFT):
             send(*fine_message(stage, direction))
+
+    def send_y_faces(stage):
         fsend[stage, UP] = pieces(
             lambda m: x_ref[:, m, 3], lambda v, m: roll_rows(v, m - 3), row4)
         fsend[stage, DOWN] = pieces(
@@ -269,7 +245,7 @@
             for a in range(5):
                 res[a, :, j, k2] = out[a]
             return c
-        lax.fori_loop(0, 8, along_x, 0)
+        repeat(8, along_x)
 
         def along_y(n, c):
             i, k2 = n // 2, n % 2
@@ -289,7 +265,7 @@
             for a in range(5):
                 res[a, i, :, k2] = out[a]
             return c
-        lax.fori_loop(0, 8, along_y, 0)
+        repeat(8, along_y)
 
         def along_z(n, c):
             i, j = n // 2, 2 * (n % 2)
@@ -321,19 +297,31 @@
             for a in range(5):
                 res[a, i, part] = out[a]
             return c
-        lax.fori_loop(0, 8, along_z, 0)
-
-    def add_halo(stage):
-        for direction in range(4):
+        repeat(8, along_z)
+
+    def add_y_halo(stage):
+        for direction in (UP, DOWN):
+            arrived(*fine_message(stage, direction))
+        from_below, from_above = frecv[stage, UP], frecv[stage, DOWN]
+        for m in range(4):
+            res[:, m, 0] = res[:, m, 0] + py_below * roll_rows(from_below, -m)
+            res[:, m, 3] = res[:, m, 3] + py_above * roll_rows(from_above, 3 - m)
+
+    def add_x_halo(stage):
+        for direction in (RIGHT, LEFT):
             arrived(*fine_message(stage, direction))
         from_left, from_right = frecv[stage, RIGHT], frecv[stage, LEFT]
-        from_below, from_above = frecv[stage, UP], frecv[stage, DOWN]
         for m in range(4):
             res[:, 0, m] = res[:, 0, m] + px_left * roll_lanes(from_left, -EZ * m)
             res[:, 3, m] = res[:, 3, m] + px_right * roll_lanes(from_right, 128 - EZ * (m + 1))
-        for m in range(4):
-            res[:, m, 0] = res[:, m, 0] + py_below * roll_rows(from_below, -m)
-            res[:, m, 3] = res[:, m, 3] + py_above * roll_rows(from_above, 3 - m)
+
+    def finish_sweep(stage, target):
+        add_y_halo(stage)
+        for i in (1, 2):
+            smooth_slab(res, i, target)
+        add_x_halo(stage)
+        for i in (0, 3):
+            smooth_slab(res, i, target)
 
     def pack_columns(value, first_block):
         quarter = value.shape[0] // 4
@@ -370,25 +358,63 @@
         return jnp.concatenate(
             [jnp.where(low_lanes, right, left), roll_lanes(jnp.where(low_lanes, left, right), 64)], axis=0)
 
-    def fill_window(window, mine, columns, rows, corners):
+    def fill_near(window, mine, rows):
         quarter = mine.shape[0] // 4
+        ends = unpack_rows(rows[0], rows[1])
+        for m in range(4):
+            part = slice(m * quarter, (m + 1) * quarter)
+            window[0, part] = jnp.where(low_half, mine[part], ends[m])
+
+    def fill_far(window, columns, corners):
+        quarter = columns[0].shape[0]
         side = unpack_columns(columns[0], columns[1])
-        ends = unpack_rows(rows[0], rows[1])
         above = unpack_corner(corners[0], corners[1])
         below = unpack_corner(corners[2], corners[3])
         edge = unpack_rows(above, below)
         for m in range(4):
-            part = slice(m * quarter, (m + 1) * quarter)
-            window[0, part] = jnp.where(low_half, mine[part], ends[m])
-            window[1, part] = jnp.where(low_half, side[m], edge[m])
+            window[1, m * quarter:(m + 1) * quarter] = jnp.where(low_half, side[m], edge[m])
 
     small[0].wait()
-    for i in range(4):
+    for i in (0, 3):
         blocks[i].wait()
-        for j in (0, 2):
-            smooth(s_ref, i, j, x_ref, True)
+        smooth_slab(s_ref, i, x_ref, True)
     pl.semaphore_wait(barrier, across * along - 1)
-    send_faces(0)
+    send_x_faces(0)
+    for i in (1, 2):
+        blocks[i].wait()
+        smooth_slab(s_ref, i, x_ref, True)
+    send_y_faces(0)
+
+    for transfer in small[1:]:
+        transfer.wait()
+    for array, start, count, scale in ((j_ref, 0, 75, 0.5), (e_ref, 75, 25, DAMPING)):
+        value = array[...]
+        jd[start:start + count, 0:4] = value
+        jd[start:start + count, 4:8] = value
+    own[0:75] = 0.5 * jd[0:75]
+    own[75:100] = DAMPING * jd[75:100]
+    for n, value in enumerate((t_ref[...], p_ref[0], p_ref[1], p_ref[2])):
+        own[100 + n, 0:4] = value
+        own[100 + n, 4:8] = value
+    time, pen_x, pen_y, pen_z = own[100], own[101], own[102], own[103]
+    for f in range(2):
+        for j in range(4):
+            for k2 in range(2):
+                total = time + pen_z * (lower if k2 == 0 else upper)
+                if j in (0, 3):
+                    total = total + pen_y
+                dg[f, j, k2] = total + pen_x if f else total
+
+    px_prior = jnp.where(lane >= EZ, pen_x, 0.0)
+    px_next = jnp.where(lane < 128 - EZ, pen_x, 0.0)
+    px_left = jnp.where(lane < EZ, pen_x, 0.0)
+    px_right = jnp.where(lane >= 128 - EZ, pen_x, 0.0)
+    py_prior = jnp.where(row4 != 0, pen_y, 0.0)
+    py_next = jnp.where(row4 != 3, pen_y, 0.0)
+    py_below = jnp.where(row4 == 0, pen_y, 0.0)
+    py_above = jnp.where(row4 == 3, pen_y, 0.0)
+    pz_prior = pen_z * lower * has_prior
+    pz_next = pen_z * upper * has_next
 
     coefficients = own[...]
     ssend[RIGHT] = pack_columns(coefficients, 1)
@@ -415,9 +441,9 @@
         clear(direction, dsrecv.at[direction - 4])
 
     residual()
-    add_halo(0)
-    smooth_all(x_ref)
-    send_faces(1)
+    finish_sweep(0, x_ref)
+    send_x_faces(1)
+    send_y_faces(1)
     residual()
     for direction in range(4):
         sent(*fine_message(0, direction))
@@ -425,12 +451,13 @@
         sent(*static_message(direction))
     for direction in range(8):
         arrived(*static_message(direction))
-    fill_window(
-        wst, own,
-        (srecv[LEFT], srecv[RIGHT]), (srecv[DOWN], srecv[UP]),
+    fill_near(wst, own, (srecv[DOWN], srecv[UP]))
+    fill_far(
+        wst, (srecv[LEFT], srecv[RIGHT]),
         (dsrecv[LEFT_DOWN - 4], dsrecv[RIGHT_DOWN - 4], dsrecv[LEFT_UP - 4], dsrecv[RIGHT_UP - 4]),
     )
-    add_halo(1)
+    add_y_halo(1)
+    add_x_halo(1)
 
     near_low, far_low = halves(1.0, NEAR), halves(FAR, 0.0)
     near_high, far_high = halves(NEAR, 1.0), halves(0.0, FAR)
@@ -452,40 +479,50 @@
                 fin[n] = z0 + roll_rows(z0, 4)
                 fin[n + 1] = z1 + roll_rows(z1, 4)
 
-    def exchange(stage, field, faces):
-        nodes = faces.reshape(5, 2, 2, 2, 8, 128)
-        x_low, x_up = nodes[:, 0].reshape(20, 8, 128), nodes[:, 1].reshape(20, 8, 128)
-        y_low, y_up = nodes[:, :, 0].reshape(20, 8, 128), nodes[:, :, 1].reshape(20, 8, 128)
-        esend[stage, RIGHT, 0:10] = pack_columns(field, 1)
-        esend[stage, RIGHT, 10:15] = pack_columns(roll_lanes(x_up, EZ), 1)
-        esend[stage, LEFT, 0:10] = pack_columns(field, 0)
-        esend[stage, LEFT, 10:15] = pack_columns(roll_lanes(x_low, -EZ), 0)
-        esend[stage, UP, 0:10] = pack_rows(field, 1)
-        esend[stage, UP, 10:15] = pack_rows(roll_rows(y_up, 1), 1)
-        esend[stage, DOWN, 0:10] = pack_rows(field, 0)
-        esend[stage, DOWN, 10:15] = pack_rows(roll_rows(y_low, -1), 0)
-        for direction, source, keep_low in (
-            (RIGHT_UP, UP, False), (RIGHT_DOWN, DOWN, False), (LEFT_UP, UP, True), (LEFT_DOWN, DOWN, True)
-        ):
-            dsend[stage, direction - 4] = pack_corner(esend[stage, source, 0:10], keep_low)
-        for direction in (4, 5, 6, 7, 0, 1, 2, 3):
+    CORNERS = ((RIGHT_UP, UP, False), (RIGHT_DOWN, DOWN, False), (LEFT_UP, UP, True), (LEFT_DOWN, DOWN, True))
+
+    def exchange(stage, field, x_prior, x_next, y_prior, y_next):
+        main = field.shape[0] // 4
+        whole = main + x_prior.shape[0] // 4
+        esend[stage, UP, 0:main] = pack_rows(field, 1)
+        esend[stage, DOWN, 0:main] = pack_rows(field, 0)
+        for direction, source, keep_low in CORNERS:
+            dsend[stage, direction - 4, 0:main // 2] = pack_corner(esend[stage, source, 0:main], keep_low)
+        for direction, _, _ in CORNERS:
             send(*coarse_message(stage, direction))
-
-    def receive(stage, window, field):
-        for direction in range(8):
+        esend[stage, RIGHT, 0:main] = pack_columns(field, 1)
+        esend[stage, RIGHT, main:whole] = pack_columns(x_prior, 1)
+        esend[stage, LEFT, 0:main] = pack_columns(field, 0)
+        esend[stage, LEFT, main:whole] = pack_columns(x_next, 0)
+        for direction in (RIGHT, LEFT):
+            send(*coarse_message(stage, direction))
+        esend[stage, UP, main:whole] = pack_rows(y_prior, 1)
+        esend[stage, DOWN, main:whole] = pack_rows(y_next, 0)
+        for direction in (UP, DOWN):
+            send(*coarse_message(stage, direction))
+
+    def receive_near(stage, window, field, strips):
+        main, more = field.shape[0] // 4, strips // 4
+        for direction in (UP, DOWN):
             arrived(*coarse_message(stage, direction))
-        fill_window(
-            window, field,
-            (erecv[stage, LEFT, 0:10], erecv[stage, RIGHT, 0:10]),
-            (erecv[stage, DOWN, 0:10], erecv[stage, UP, 0:10]),
-            (drecv[stage, LEFT_DOWN - 4], drecv[stage, RIGHT_DOWN - 4],
-             drecv[stage, LEFT_UP - 4], drecv[stage, RIGHT_UP - 4]),
+        fill_near(window, field, (erecv[stage, DOWN, 0:main], erecv[stage, UP, 0:main]))
+        ends = unpack_rows(erecv[stage, DOWN, main:main + more], erecv[stage, UP, main:main + more])
+        for m in range(4):
+            wry[more * m:more * m + more] = ends[m]
+
+    def receive_far(stage, window, fields, strips):
+        main, more = fields // 4, strips // 4
+        for direction in (RIGHT, LEFT, RIGHT_UP, RIGHT_DOWN, LEFT_UP, LEFT_DOWN):
+            arrived(*coarse_message(stage, direction))
+        half = main // 2
+        fill_far(
+            window, (erecv[stage, LEFT, 0:main], erecv[stage, RIGHT, 0:main]),
+            (drecv[stage, LEFT_DOWN - 4, 0:half], drecv[stage, RIGHT_DOWN - 4, 0:half],
+             drecv[stage, LEFT_UP - 4, 0:half], drecv[stage, RIGHT_UP - 4, 0:half]),
         )
-        side = unpack_columns(erecv[stage, LEFT, 10:15], erecv[stage, RIGHT, 10:15])
-        ends = unpack_rows(erecv[stage, DOWN, 10:15], erecv[stage, UP, 10:15])
-        for m in range(4):
-            wrx[5 * m:5 * m + 5] = side[m]
-            wry[5 * m:5 * m + 5] = ends[m]
+        side = unpack_columns(erecv[stage, LEFT, main:main + more], erecv[stage, RIGHT, main:main + more])
+        for m in range(4):
+            wrx[more * m:more * m + more] = side[m]
 
     strip_right = jnp.logical_and(low_half, lane // EZ == 1)
     strip_left = jnp.logical_and(low_half, lane // EZ == 2)
@@ -521,42 +558,32 @@
             y = (py * (y_low[tile] - y_prior), py * (y_up[tile] - y_next))
             z = (pz * (z_low[tile] - has_prior * roll_lanes(z_up[tile], 1)),
                  pz * (z_up[tile] - has_next * roll_lanes(z_low[tile], -1)))
-            slopes = (x_up[tile] - x_low[tile], y_up[tile] - y_low[tile], z_up[tile] - z_low[tile])
-            out.append((tiles[tile], x, y, z, slopes))
+            out.append((tiles[tile], x, y, z))
         return out
 
-    def fluxes(tiles):
-        def one(n, c):
-            d, tile = n // tiles, n % tiles
-            slopes = [wsl[tile, d, b] for b in range(5)]
-            totals = []
+    def fluxes(tile):
+        slopes = ([], [], [])
+        for a in range(5):
+            u = wm[tile, a * 8:a * 8 + 8].reshape(2, 2, 2, 8, 128)
+            slopes[0].append((u[1] - u[0]).reshape(4, 8, 128))
+            slopes[1].append((u[:, 1] - u[:, 0]).reshape(4, 8, 128))
+            slopes[2].append((u[:, :, 1] - u[:, :, 0]).reshape(4, 8, 128))
+        for d in range(3):
             for a in range(5):
-                total = wst[tile, d * 25 + a * 5] * slopes[0]
+                total = wst[tile, d * 25 + a * 5] * slopes[d][0]
                 for b in range(1, 5):
-                    total = total + wst[tile, d * 25 + a * 5 + b] * slopes[b]
-                totals.append(total)
-            for a in range(5):
-                wc[tile, d, a] = totals[a]
-            return c
-        lax.fori_loop(0, 3 * tiles, one, 0)
-
-    def middle_residual(use_strips):
-        def one(a, c):
-            rest = []
-            for tile, (u, x, y, z, slopes) in enumerate(window_faces(a, use_strips)):
-                r = ws[tile, pl.ds(a * 8, 8)] - wst[tile, 100] * u
+                    total = total + wst[tile, d * 25 + a * 5 + b] * slopes[d][b]
+                wc[tile, d, a] = total
+
+    def middle_faces(use_strips):
+        for a in range(5):
+            for tile, (u, x, y, z) in enumerate(window_faces(a, use_strips)):
+                r = ws[tile, a * 8:a * 8 + 8] - wst[tile, 100] * u
                 r = r.reshape(2, 2, 2, 8, 128)
                 r = r - jnp.stack(x, axis=0).reshape(2, 2, 2, 8, 128)
                 r = r - jnp.stack([v.reshape(2, 2, 8, 128) for v in y], axis=1)
                 r = r - jnp.stack([v.reshape(2, 2, 8, 128) for v in z], axis=2)
-                rest.append((r.reshape(8, 8, 128), slopes))
-            for tile, (r, slopes) in enumerate(rest):
-                wres[tile, a] = r
-                for d in range(3):
-                    wsl[tile, d, a] = slopes[d]
-            return c
-        lax.fori_loop(0, 5, one, 0)
-        fluxes(2)
+                wres[tile, a] = r.reshape(8, 8, 128)
 
     def full_residual(tile, ip, a):
         r = wres[tile, a, pl.ds(ip * 4, 4)].reshape(2, 2, 8, 128)
@@ -573,48 +600,54 @@
             out.append(total)
         return out
 
-    def middle_sweep(use_strips):
-        middle_residual(use_strips)
-
-        def one(n, c):
-            tile, ip = n // 2, n % 2
-            r = [full_residual(tile, ip, a).reshape(4, 8, 128) for a in range(5)]
-            parts = [pl.ds(a * 8 + ip * 4, 4) for a in range(5)]
-            totals = [wm[tile, part] + change for part, change in zip(parts, element_product(tile, r))]
-            for part, total in zip(parts, totals):
-                wm[tile, part] = total
-            return c
-        lax.fori_loop(0, 4, one, 0)
-
-    def own_guess(n, c):
-        part = [fin[pl.ds(b * 8 + n * 4, 4)] for b in range(5)]
+    def middle_update():
+        for tile in range(2):
+            for ip in range(2):
+                r = [full_residual(tile, ip, a).reshape(4, 8, 128) for a in range(5)]
+                parts = [pl.ds(a * 8 + ip * 4, 4) for a in range(5)]
+                for part, change in zip(parts, element_product(tile, r)):
+                    wm[tile, part] = wm[tile, part] + change
+
+    def first_guess(tile):
+        for ip in range(2):
+            part = [ws[tile, pl.ds(b * 8 + ip * 4, 4)] for b in range(5)]
+            for a, value in enumerate(element_product(tile, part)):
+                wm[tile, pl.ds(a * 8 + ip * 4, 4)] = value
+
+    for ip in range(2):
+        part = [fin[pl.ds(b * 8 + ip * 4, 4)] for b in range(5)]
         for a, value in enumerate(element_product(0, part)):
-            fin[pl.ds(40 + a * 8 + n * 4, 4)] = value
-        return c
-    lax.fori_loop(0, 2, own_guess, 0)
-    exchange(0, fin[0:40], fin[40:80])
-    receive(0, ws, fin[0:40])
-
-    def first_guess(n, c):
-        tile, ip = n // 2, n % 2
-        part = [ws[tile, pl.ds(b * 8 + ip * 4, 4)] for b in range(5)]
-        for a, value in enumerate(element_product(tile, part)):
-            wm[tile, pl.ds(a * 8 + ip * 4, 4)] = value
-        return c
-    lax.fori_loop(0, 4, first_guess, 0)
-    middle_sweep(True)
-    middle_residual(False)
-
+            fin[pl.ds(40 + a * 8 + ip * 4, 4)] = value
+    nodes = fin[40:80].reshape(5, 2, 2, 2, 8, 128)
+    exchange(
+        0, fin[0:40],
+        roll_lanes(nodes[:, 1].reshape(20, 8, 128), EZ), roll_lanes(nodes[:, 0].reshape(20, 8, 128), -EZ),
+        roll_rows(nodes[:, :, 1].reshape(20, 8, 128), 1), roll_rows(nodes[:, :, 0].reshape(20, 8, 128), -1),
+    )
+    receive_near(0, ws, fin[0:40], 20)
+    first_guess(0)
+    fluxes(0)
+    receive_far(0, ws, 40, 20)
+    first_guess(1)
+    fluxes(1)
+    middle_faces(True)
+    middle_update()
     for tile in range(2):
-        def bottom_source(a, c, tile=tile):
-            total = full_residual(tile, 0, a) + full_residual(tile, 1, a)
+        fluxes(tile)
+    middle_faces(False)
+
+    for tile in range(2):
+        source = []
+        for a in range(5):
+            parts = [full_residual(tile, ip, a) for ip in range(2)]
+            if tile == 0:
+                for ip in range(2):
+                    fin[a * 8 + ip * 4:a * 8 + ip * 4 + 4] = parts[ip].reshape(4, 8, 128)
+            total = parts[0] + parts[1]
             total = total[0] + total[1]
-            wb[0, tile, a] = total[0] + total[1]
-            return c
-        lax.fori_loop(0, 5, bottom_source, 0)
-    for tile in range(2):
-        values = [wb[0, tile, a] for a in range(5)]
-        for a, value in enumerate(element_product(tile, values)):
+            source.append(total[0] + total[1])
+            wb[0, tile, a] = source[a]
+        for a, value in enumerate(element_product(tile, source)):
             wb[1, tile, a] = value
     bottom = wb[1, 0]
     (x_next, _), (x_prior, _) = across_x(bottom, wb[1, 1], bottom, wb[1, 1], None)
@@ -625,24 +658,64 @@
     rest = wb[0, 0] - applied
     change = element_product(0, [rest[b] for b in range(5)])
     for a in range(5):
-        fin[a * 8:a * 8 + 8] = wm[0, a * 8:a * 8 + 8] + (bottom[a] + change[a])
-
-    exchange(1, fin[0:40], fin[0:40])
-    receive(1, wm, fin[0:40])
-    middle_sweep(True)
-    middle_sweep(False)
+        fin[40 + a] = bottom[a] + change[a]
+    for n in range(45, 48):
+        fin[n] = jnp.zeros((8, 128), F32)
+
+    guess = fin[40:48]
+    exchange(
+        1, fin[0:48], roll_lanes(guess, EZ), roll_lanes(guess, -EZ), roll_rows(guess, 1), roll_rows(guess, -1))
+
+    def constant_terms(tile, b, y_next, y_prior):
+        py, pz = wst[tile, 102], wst[tile, 103]
+        y = (py * (b - y_prior), py * (b - y_next))
+        z = (pz * (b - has_prior * roll_lanes(b, 1)), pz * (b - has_next * roll_lanes(b, -1)))
+        base = wst[tile, 100] * b
+        return [[(base + y[jp]) + z[kp] for kp in range(2)] for jp in range(2)]
+
+    def add_bottom(tile, b, terms, x_terms):
+        for ip in range(2):
+            r = []
+            for a in range(5):
+                own_terms = jnp.stack([terms[jp][kp][a] for jp in range(2) for kp in range(2)])
+                value = w48[tile, a * 8 + ip * 4:a * 8 + ip * 4 + 4] - own_terms
+                r.append(value if x_terms is None else value - x_terms[ip][a])
+            for a, change in enumerate(element_product(tile, r)):
+                part = pl.ds(a * 8 + ip * 4, 4)
+                wm[tile, part] = wm[tile, part] + (b[a] + change)
+
+    receive_near(1, w48, fin[0:48], 8)
+    b0 = w48[0, 40:45]
+    y_next = jnp.where(row == 5, wry[0:5], roll_rows(b0, -1))
+    y_prior = jnp.where(row == 6, wry[0:5], roll_rows(b0, 1))
+    add_bottom(0, b0, constant_terms(0, b0, y_next, y_prior), None)
+    receive_far(1, w48, 48, 8)
+    b1 = w48[1, 40:45]
+    x_next, x_prior = across_x(b0, b1, b0, b1, wrx[0:5])
+    x_terms = [
+        (wst[tile, 101] * (b - x_prior[tile]), wst[tile, 101] * (b - x_next[tile]))
+        for tile, b in enumerate((b0, b1))
+    ]
+    for ip in range(2):
+        change = element_product(0, [x_terms[0][ip][a] for a in range(5)])
+        for a in range(5):
+            part = pl.ds(a * 8 + ip * 4, 4)
+            wm[0, part] = wm[0, part] - change[a]
+    add_bottom(1, b1, constant_terms(1, b1, roll_rows(b1, -1), roll_rows(b1, 1)), x_terms[1])
+    for tile in range(2):
+        fluxes(tile)
+    middle_faces(False)
+    middle_update()
 
     def final_parts(a, c):
-        u, x, y, z, slopes = window_faces(a, False)[0]
-        for d in range(3):
-            wsl[0, d, a] = slopes[d]
+        u, x, y, z = window_faces(a, False)[0]
         wres[0, a] = wst[0, 100] * u
         for d, terms in enumerate((x, y, z)):
             for side in range(2):
-                fin[pl.ds((d * 2 + side) * 20 + a * 4, 4)] = terms[side]
-        return c
-    lax.fori_loop(0, 5, final_parts, 0)
-    fluxes(1)
+                fin[(d * 2 + side) * 20 + a * 4:(d * 2 + side) * 20 + a * 4 + 4] = terms[side]
+    for a in range(5):
+        final_parts(a, 0)
+    fluxes(0)
 
     def both(value):
         return jnp.where(low_half, value, roll_rows(value, 4))
@@ -656,57 +729,64 @@
     def spread_line(v0, v1):
         return v0, NEAR * v0 + FAR * v1, FAR * v0 + NEAR * v1, v1
 
-    def prolong(value):
+    def prolong_lines(value):
         value = both(value)
         z0, z1 = spread_z(value[:, :, 0], value[:, :, 1])
         pairs = jnp.stack([z0, z1], axis=2)
-        lines = jnp.stack(spread_line(pairs[:, 0], pairs[:, 1]), axis=1)
-        return spread_line(lines[0], lines[1])
-
-    def final_fine(a, c):
-        guess = [x_ref[a, i] + value
-                 for i, value in enumerate(prolong(wm[0, pl.ds(a * 8, 8)].reshape(2, 2, 2, 8, 128)))]
+        return jnp.stack(spread_line(pairs[:, 0], pairs[:, 1]), axis=1)
+
+    def between(lines, i):
+        if i in (0, 3):
+            return lines[i // 3]
+        near, far = (0, 1) if i == 1 else (1, 0)
+        return NEAR * lines[near] + FAR * lines[far]
+
+    def face_lines(a, d, side):
+        face = both(fin[(d * 2 + side) * 20 + a * 4:(d * 2 + side) * 20 + a * 4 + 4].reshape(2, 2, 8, 128))
+        return jnp.stack(spread_z(face[:, 0], face[:, 1]), axis=1)
+
+    def final_slabs(slabs):
+        for a in range(5):
+            guess, volume = lines_of[a]
+            y_faces, z_faces = faces_of[a]
+            for i in slabs:
+                x_ref[a, i] = x_ref[a, i] + between(guess, i)
+                value = res[a, i] - between(volume, i)
+                if i in (0, 3):
+                    z = face_lines(a, 0, i // 3)
+                    value = value - jnp.stack(spread_line(z[0], z[1]))
+                y = [between(face, i) for face in y_faces]
+                z = jnp.stack([between(face, i) for face in z_faces], axis=1)
+                value = value - z
+                res[a, i] = jnp.concatenate([(value[0] - y[0])[None], value[1:3], (value[3] - y[1])[None]])
+
+    lines_of, faces_of = [], []
+    for a in range(5):
         volume = wres[0, a].reshape(2, 2, 2, 8, 128) + wc[0, 0, a].reshape(1, 2, 2, 8, 128)
         volume = volume + wc[0, 1, a].reshape(2, 1, 2, 8, 128) + wc[0, 2, a].reshape(2, 2, 1, 8, 128)
-        rest = [[[res[a, i, j, k2] - value[j, k2] for k2 in range(2)] for j in range(4)]
-                for i, value in enumerate(prolong(volume))]
+        lines_of.append((prolong_lines(wm[0, a * 8:a * 8 + 8].reshape(2, 2, 2, 8, 128)), prolong_lines(volume)))
+        y_faces = [face_lines(a, 1, side) for side in range(2)]
+        z_faces = []
         for side in range(2):
-            end = 3 * side
-            face = both(fin[pl.ds(side * 20 + a * 4, 4)].reshape(2, 2, 8, 128))
-            z = jnp.stack(spread_z(face[:, 0], face[:, 1]), axis=1)
-            for m, value in enumerate(spread_line(z[0], z[1])):
-                for k2 in range(2):
-                    rest[end][m][k2] = rest[end][m][k2] - value[k2]
-            face = both(fin[pl.ds((2 + side) * 20 + a * 4, 4)].reshape(2, 2, 8, 128))
-            z = jnp.stack(spread_z(face[:, 0], face[:, 1]), axis=1)
-            for m, value in enumerate(spread_line(z[0], z[1])):
-                for k2 in range(2):
-                    rest[m][end][k2] = rest[m][end][k2] - value[k2]
-            face = fin[pl.ds((4 + side) * 20 + a * 4, 4)].reshape(2, 2, 8, 128)
+            face = fin[(4 + side) * 20 + a * 4:(4 + side) * 20 + a * 4 + 4].reshape(2, 2, 8, 128)
             face = lower * face if side == 0 else upper * roll_rows(face, 4)
-            lines = jnp.stack(spread_line(face[:, 0], face[:, 1]), axis=1)
-            for m, value in enumerate(spread_line(lines[0], lines[1])):
-                for n in range(4):
-                    rest[m][n][side] = rest[m][n][side] - value[n]
-        for i in range(4):
-            x_ref[a, i] = guess[i]
-            for j in range(4):
-                for k2 in range(2):
-                    res[a, i, j, k2] = rest[i][j][k2]
-        return c
-    lax.fori_loop(0, 5, final_fine, 0)
-    smooth_all(x_ref)
-
-    send_faces(2)
+            z_faces.append(jnp.stack(spread_line(face[:, 0], face[:, 1]), axis=1))
+        faces_of.append((y_faces, z_faces))
+    final_slabs((0, 3))
+    for i in (0, 3):
+        smooth_slab(res, i, x_ref)
+    send_x_faces(2)
+    final_slabs((1, 2))
+    for i in (1, 2):
+        smooth_slab(res, i, x_ref)
+    send_y_faces(2)
     residual()
     for stage in range(2):
         for direction in range(8):
             sent(*coarse_message(stage, direction))
     for direction in range(4):
         sent(*fine_message(1, direction))
-    add_halo(2)
-    smooth_all(out_ref)
-
+    finish_sweep(2, out_ref)
     for direction in range(4):
         sent(*fine_message(2, direction))
 
@@ -730,8 +810,8 @@
                 pltpu.VMEM((3, 4, 128), F32), pltpu.VMEM((25, 4, 128), F32),
                 vmem(5, 4, 4, 2), vmem(100), vmem(104), vmem(2, 4, 2), vmem(5, 4, 4, 2),
                 vmem(3, 4, 5, 2), vmem(3, 4, 5, 2), vmem(4, 26), vmem(4, 26),
-                vmem(2, 4, 15), vmem(2, 4, 15), vmem(2, 4, 5), vmem(2, 4, 5), vmem(4, 13), vmem(4, 13),
-                vmem(2, 104), vmem(2, 40), vmem(2, 40), vmem(2, 5, 8), vmem(2, 3, 5, 4), vmem(2, 3, 5, 4),
+                vmem(2, 4, 15), vmem(2, 4, 15), vmem(2, 4, 6), vmem(2, 4, 6), vmem(4, 13), vmem(4, 13),
+                vmem(2, 104), vmem(2, 40), vmem(2, 40), vmem(2, 48), vmem(2, 5, 8), vmem(2, 3, 5, 4),
                 vmem(20), vmem(20), vmem(2, 2, 5), vmem(120),
                 dma(3, 4), dma(3, 4), dma(8), dma(8), dma(2, 8), dma(2, 8), dma(9),
             ],

time: 35.8 us -> 31.8 us (0.89)
  Pallas kernels: 34.8 us -> 30.9 us
    pallas_call x1, Pallas kernels: 34.8 us -> 30.9 us  [on_device(): pl.pallas_call(run, out_shape=jax.ShapeDtypeStruct((5, 4, 4, 2, 8, 128),...]
where the time goes in v2:
time: 31.8 us; the launch traced here: 31.7 us
  Pallas kernels  30.9 us (97%)
  local copies, waits for them, and re-layouts  0.84 us (3%)
    pallas_call x1, Pallas kernels, on_device(): pl.pallas_call(run, out_shape=jax.ShapeDtypeStruct((5, 4, 4, 2, 8, 128),...  30.9 us
    unnamed x1, local copies, waits for them, and re-layouts  0.84 us

profile of v2, /device:TPU:6, one launch (start us, length us, event | category | flops | bytes accessed | tf_op | source)
XLA Modules:
  0.0 31.7 jit_solution(14799087038224585611)
XLA Ops:
  0.0 30.9 %shard_map.64 = f32[5,4,4,2,8,128]{5,4,3,2,1,0:T(8,128)S(1)} custom-call(f32[5,4,4,2,8,128]{5,4,3,2,1,0:T(8,128)} %bitcast.7, f32[5,5,4,4,2,8,128]{6,5,4,3,2,1,0:T(8,128)} %bitcast.6, f32[75,4,128]{2,1,0:T(4,128)} %bitcast.8, f32[4,128]{1,0:T(4,128)} %refs_3_.1, f32[3,4,128]{2,1,0:T(4,128)} %refs_4_.1, f32[25,4,128]{2,1,0:T(4,128)} %bitcast.9), custom_call_target="tpu_custom_call" | custom-call | tf_op jit(solution)/shard_map/pallas_call | solution.py:803
  30.9 0.8 %copy.8 = f32[5,64,4,128]{3,2,1,0:T(4,128)} copy(f32[5,64,4,128]{3,2,1,0:T(4,128)S(1)} %bitcast.5) | data formatting | bytes 1310720

commit v3 on v2

--- a/solution.py
+++ b/solution.py
@@ -57,7 +57,7 @@
     s_ref, b_ref, j_ref, t_ref, p_ref, e_ref,
     x_ref, jd, own, dg, res,
     fsend, frecv, ssend, srecv, esend, erecv, dsend, drecv, dssend, dsrecv,
-    wst, wm, ws, w48, wres, wc, wrx, wry, wb, fin,
+    wst, wdg, wm, ws, w48, wres, wc, wrx, wry, wb, fin,
     f_ss, f_rs, s_ss, s_rs, e_ss, e_rs, in_sem,
 ):
     small = [
@@ -456,6 +456,11 @@
         wst, (srecv[LEFT], srecv[RIGHT]),
         (dsrecv[LEFT_DOWN - 4], dsrecv[RIGHT_DOWN - 4], dsrecv[LEFT_UP - 4], dsrecv[RIGHT_UP - 4]),
     )
+    for tile in range(2):
+        px, py, pz = wst[tile, 101], wst[tile, 102], wst[tile, 103]
+        wdg[tile, 0] = wst[tile, 100] + (px + py + pz)
+        wdg[tile, 1] = pz * has_prior
+        wdg[tile, 2] = pz * has_next
     add_y_halo(1)
     add_x_halo(1)
 
@@ -538,27 +543,26 @@
             prior1 = jnp.where(strip_left, strip, prior1)
         return (next0, next1), (prior0, prior1)
 
-    def window_faces(a, use_strips):
-        tiles = [wm[tile, pl.ds(a * 8, 8)] for tile in range(2)]
+    def neighbours(a, use_strips):
+        tiles = [wm[tile, a * 8:a * 8 + 8] for tile in range(2)]
         nodes = [u.reshape(2, 2, 2, 8, 128) for u in tiles]
         x_low, x_up = [u[0].reshape(4, 8, 128) for u in nodes], [u[1].reshape(4, 8, 128) for u in nodes]
         y_low, y_up = [u[:, 0].reshape(4, 8, 128) for u in nodes], [u[:, 1].reshape(4, 8, 128) for u in nodes]
         z_low, z_up = [u[:, :, 0].reshape(4, 8, 128) for u in nodes], [u[:, :, 1].reshape(4, 8, 128) for u in nodes]
         x_next, x_prior = across_x(
-            x_low[0], x_low[1], x_up[0], x_up[1], wrx[pl.ds(a * 4, 4)] if use_strips else None)
+            x_low[0], x_low[1], x_up[0], x_up[1], wrx[a * 4:a * 4 + 4] if use_strips else None)
         out = []
         for tile in range(2):
-            px, py, pz = wst[tile, 101], wst[tile, 102], wst[tile, 103]
-            x = (px * (x_low[tile] - x_prior[tile]), px * (x_up[tile] - x_next[tile]))
             y_next, y_prior = roll_rows(y_low[tile], -1), roll_rows(y_up[tile], 1)
             if tile == 0 and use_strips:
-                strip = wry[pl.ds(a * 4, 4)]
+                strip = wry[a * 4:a * 4 + 4]
                 y_next = jnp.where(row == 5, strip, y_next)
                 y_prior = jnp.where(row == 6, strip, y_prior)
-            y = (py * (y_low[tile] - y_prior), py * (y_up[tile] - y_next))
-            z = (pz * (z_low[tile] - has_prior * roll_lanes(z_up[tile], 1)),
-                 pz * (z_up[tile] - has_next * roll_lanes(z_low[tile], -1)))
-            out.append((tiles[tile], x, y, z))
+            out.append((
+                tiles[tile], (x_prior[tile], x_next[tile]), (y_prior, y_next),
+                (roll_lanes(z_up[tile], 1), roll_lanes(z_low[tile], -1)),
+                ((x_low[tile], x_up[tile]), (y_low[tile], y_up[tile]), (z_low[tile], z_up[tile])),
+            ))
         return out
 
     def fluxes(tile):
@@ -575,14 +579,15 @@
                     total = total + wst[tile, d * 25 + a * 5 + b] * slopes[d][b]
                 wc[tile, d, a] = total
 
-    def middle_faces(use_strips):
-        for a in range(5):
-            for tile, (u, x, y, z) in enumerate(window_faces(a, use_strips)):
-                r = ws[tile, a * 8:a * 8 + 8] - wst[tile, 100] * u
-                r = r.reshape(2, 2, 2, 8, 128)
-                r = r - jnp.stack(x, axis=0).reshape(2, 2, 2, 8, 128)
-                r = r - jnp.stack([v.reshape(2, 2, 8, 128) for v in y], axis=1)
-                r = r - jnp.stack([v.reshape(2, 2, 8, 128) for v in z], axis=2)
+    def middle_faces(use_strips, tiles=2):
+        for a in range(5):
+            for tile, (u, x, y, z, _) in enumerate(neighbours(a, use_strips)[:tiles]):
+                px, py = wst[tile, 101], wst[tile, 102]
+                pz = (wdg[tile, 1], wdg[tile, 2])
+                r = (ws[tile, a * 8:a * 8 + 8] - wdg[tile, 0] * u).reshape(2, 2, 2, 8, 128)
+                r = r + jnp.stack([px * v for v in x], axis=0).reshape(2, 2, 2, 8, 128)
+                r = r + jnp.stack([(py * v).reshape(2, 2, 8, 128) for v in y], axis=1)
+                r = r + jnp.stack([(p * v).reshape(2, 2, 8, 128) for p, v in zip(pz, z)], axis=2)
                 wres[tile, a] = r.reshape(8, 8, 128)
 
     def full_residual(tile, ip, a):
@@ -632,20 +637,51 @@
     fluxes(1)
     middle_faces(True)
     middle_update()
-    for tile in range(2):
-        fluxes(tile)
-    middle_faces(False)
-
-    for tile in range(2):
+    fluxes(0)
+    middle_faces(False, 1)
+
+    def far_sources():
+        rest, slopes = [], ([], [], [])
+        for a in range(5):
+            u = wm[1, a * 8:a * 8 + 8].reshape(2, 2, 2, 8, 128)
+            v = wm[0, a * 8:a * 8 + 8].reshape(2, 4, 8, 128)
+            pairs = u[:, :, 0] + u[:, :, 1]
+            x_low, x_up = pairs[0, 0] + pairs[0, 1], pairs[1, 0] + pairs[1, 1]
+            y_low, y_up = pairs[0, 0] + pairs[1, 0], pairs[0, 1] + pairs[1, 1]
+            z = u[0] + u[1]
+            z_low, z_up = z[0, 0] + z[1, 0], z[0, 1] + z[1, 1]
+            near_low = (v[0, 0] + v[0, 1]) + (v[0, 2] + v[0, 3])
+            near_up = (v[1, 0] + v[1, 1]) + (v[1, 2] + v[1, 3])
+            (_, x_next), (_, x_prior) = across_x(near_low, x_low, near_up, x_up, None)
+            total = ws[1, a * 8]
+            for n in range(1, 8):
+                total = total + ws[1, a * 8 + n]
+            total = total - wdg[1, 0] * (x_low + x_up)
+            total = total + wst[1, 101] * (x_next + x_prior)
+            total = total + wst[1, 102] * (roll_rows(y_low, -1) + roll_rows(y_up, 1))
+            total = total + (wdg[1, 1] * roll_lanes(z_up, 1) + wdg[1, 2] * roll_lanes(z_low, -1))
+            rest.append(total)
+            for d, slope in enumerate((x_up - x_low, y_up - y_low, z_up - z_low)):
+                slopes[d].append(2.0 * slope)
+        for a in range(5):
+            for d in range(3):
+                for b in range(5):
+                    rest[a] = rest[a] - wst[1, d * 25 + a * 5 + b] * slopes[d][b]
+        return rest
+
+    def near_sources():
         source = []
         for a in range(5):
-            parts = [full_residual(tile, ip, a) for ip in range(2)]
-            if tile == 0:
-                for ip in range(2):
-                    fin[a * 8 + ip * 4:a * 8 + ip * 4 + 4] = parts[ip].reshape(4, 8, 128)
+            parts = [full_residual(0, ip, a) for ip in range(2)]
+            for ip in range(2):
+                fin[a * 8 + ip * 4:a * 8 + ip * 4 + 4] = parts[ip].reshape(4, 8, 128)
             total = parts[0] + parts[1]
             total = total[0] + total[1]
             source.append(total[0] + total[1])
+        return source
+
+    for tile, source in enumerate((near_sources(), far_sources())):
+        for a in range(5):
             wb[0, tile, a] = source[a]
         for a, value in enumerate(element_product(tile, source)):
             wb[1, tile, a] = value
@@ -669,9 +705,9 @@
     def constant_terms(tile, b, y_next, y_prior):
         py, pz = wst[tile, 102], wst[tile, 103]
         y = (py * (b - y_prior), py * (b - y_next))
-        z = (pz * (b - has_prior * roll_lanes(b, 1)), pz * (b - has_next * roll_lanes(b, -1)))
-        base = wst[tile, 100] * b
-        return [[(base + y[jp]) + z[kp] for kp in range(2)] for jp in range(2)]
+        base = (wst[tile, 100] + pz) * b
+        z = (base - wdg[tile, 1] * roll_lanes(b, 1), base - wdg[tile, 2] * roll_lanes(b, -1))
+        return [[y[jp] + z[kp] for kp in range(2)] for jp in range(2)]
 
     def add_bottom(tile, b, terms, x_terms):
         for ip in range(2):
@@ -708,11 +744,13 @@
     middle_update()
 
     def final_parts(a, c):
-        u, x, y, z = window_faces(a, False)[0]
+        u, x, y, z, own_sides = neighbours(a, False)[0]
         wres[0, a] = wst[0, 100] * u
-        for d, terms in enumerate((x, y, z)):
+        for d, others in enumerate((x, y, z)):
             for side in range(2):
-                fin[(d * 2 + side) * 20 + a * 4:(d * 2 + side) * 20 + a * 4 + 4] = terms[side]
+                p = wst[0, 101 + d]
+                value = p * own_sides[d][side] - (wdg[0, 1 + side] if d == 2 else p) * others[side]
+                fin[(d * 2 + side) * 20 + a * 4:(d * 2 + side) * 20 + a * 4 + 4] = value
     for a in range(5):
         final_parts(a, 0)
     fluxes(0)
@@ -811,7 +849,7 @@
                 vmem(5, 4, 4, 2), vmem(100), vmem(104), vmem(2, 4, 2), vmem(5, 4, 4, 2),
                 vmem(3, 4, 5, 2), vmem(3, 4, 5, 2), vmem(4, 26), vmem(4, 26),
                 vmem(2, 4, 15), vmem(2, 4, 15), vmem(2, 4, 6), vmem(2, 4, 6), vmem(4, 13), vmem(4, 13),
-                vmem(2, 104), vmem(2, 40), vmem(2, 40), vmem(2, 48), vmem(2, 5, 8), vmem(2, 3, 5, 4),
+                vmem(2, 104), vmem(2, 3), vmem(2, 40), vmem(2, 40), vmem(2, 48), vmem(2, 5, 8), vmem(2, 3, 5, 4),
                 vmem(20), vmem(20), vmem(2, 2, 5), vmem(120),
                 dma(3, 4), dma(3, 4), dma(8), dma(8), dma(2, 8), dma(2, 8), dma(9),
             ],

time: 31.8 us -> 31.6 us (level)
  no operation moved by 1% of the time
where the time goes in v3:
time: 31.6 us; the launch traced here: 31.5 us
  Pallas kernels  30.7 us (97%)
  local copies, waits for them, and re-layouts  0.84 us (3%)
    pallas_call x1, Pallas kernels, on_device(): pl.pallas_call(run, out_shape=jax.ShapeDtypeStruct((5, 4, 4, 2, 8, 128),...  30.7 us
    unnamed x1, local copies, waits for them, and re-layouts  0.84 us

profile of v3, /device:TPU:6, one launch (start us, length us, event | category | flops | bytes accessed | tf_op | source)
XLA Modules:
  0.0 31.5 jit_solution(11490175400230867636)
XLA Ops:
  0.0 30.7 %shard_map.64 = f32[5,4,4,2,8,128]{5,4,3,2,1,0:T(8,128)S(1)} custom-call(f32[5,4,4,2,8,128]{5,4,3,2,1,0:T(8,128)} %bitcast.7, f32[5,5,4,4,2,8,128]{6,5,4,3,2,1,0:T(8,128)} %bitcast.6, f32[75,4,128]{2,1,0:T(4,128)} %bitcast.8, f32[4,128]{1,0:T(4,128)} %refs_3_.1, f32[3,4,128]{2,1,0:T(4,128)} %refs_4_.1, f32[25,4,128]{2,1,0:T(4,128)} %bitcast.9), custom_call_target="tpu_custom_call" | custom-call | tf_op jit(solution)/shard_map/pallas_call | solution.py:841
  30.7 0.8 %copy.8 = f32[5,64,4,128]{3,2,1,0:T(4,128)} copy(f32[5,64,4,128]{3,2,1,0:T(4,128)S(1)} %bitcast.5) | data formatting | bytes 1310720

commit v4 on v3

--- a/solution.py
+++ b/solution.py
@@ -486,15 +486,16 @@
 
     CORNERS = ((RIGHT_UP, UP, False), (RIGHT_DOWN, DOWN, False), (LEFT_UP, UP, True), (LEFT_DOWN, DOWN, True))
 
-    def exchange(stage, field, x_prior, x_next, y_prior, y_next):
+    def exchange(stage, field, strips):
         main = field.shape[0] // 4
-        whole = main + x_prior.shape[0] // 4
         esend[stage, UP, 0:main] = pack_rows(field, 1)
         esend[stage, DOWN, 0:main] = pack_rows(field, 0)
         for direction, source, keep_low in CORNERS:
             dsend[stage, direction - 4, 0:main // 2] = pack_corner(esend[stage, source, 0:main], keep_low)
         for direction, _, _ in CORNERS:
             send(*coarse_message(stage, direction))
+        x_prior, x_next, y_prior, y_next = strips()
+        whole = main + x_prior.shape[0] // 4
         esend[stage, RIGHT, 0:main] = pack_columns(field, 1)
         esend[stage, RIGHT, main:whole] = pack_columns(x_prior, 1)
         esend[stage, LEFT, 0:main] = pack_columns(field, 0)
@@ -619,16 +620,17 @@
             for a, value in enumerate(element_product(tile, part)):
                 wm[tile, pl.ds(a * 8 + ip * 4, 4)] = value
 
-    for ip in range(2):
-        part = [fin[pl.ds(b * 8 + ip * 4, 4)] for b in range(5)]
-        for a, value in enumerate(element_product(0, part)):
-            fin[pl.ds(40 + a * 8 + ip * 4, 4)] = value
-    nodes = fin[40:80].reshape(5, 2, 2, 2, 8, 128)
-    exchange(
-        0, fin[0:40],
-        roll_lanes(nodes[:, 1].reshape(20, 8, 128), EZ), roll_lanes(nodes[:, 0].reshape(20, 8, 128), -EZ),
-        roll_rows(nodes[:, :, 1].reshape(20, 8, 128), 1), roll_rows(nodes[:, :, 0].reshape(20, 8, 128), -1),
-    )
+    def own_strips():
+        for ip in range(2):
+            part = [fin[pl.ds(b * 8 + ip * 4, 4)] for b in range(5)]
+            for a, value in enumerate(element_product(0, part)):
+                fin[pl.ds(40 + a * 8 + ip * 4, 4)] = value
+        nodes = fin[40:80].reshape(5, 2, 2, 2, 8, 128)
+        return (
+            roll_lanes(nodes[:, 1].reshape(20, 8, 128), EZ), roll_lanes(nodes[:, 0].reshape(20, 8, 128), -EZ),
+            roll_rows(nodes[:, :, 1].reshape(20, 8, 128), 1), roll_rows(nodes[:, :, 0].reshape(20, 8, 128), -1),
+        )
+    exchange(0, fin[0:40], own_strips)
     receive_near(0, ws, fin[0:40], 20)
     first_guess(0)
     fluxes(0)
@@ -700,7 +702,8 @@
 
     guess = fin[40:48]
     exchange(
-        1, fin[0:48], roll_lanes(guess, EZ), roll_lanes(guess, -EZ), roll_rows(guess, 1), roll_rows(guess, -1))
+        1, fin[0:48],
+        lambda: (roll_lanes(guess, EZ), roll_lanes(guess, -EZ), roll_rows(guess, 1), roll_rows(guess, -1)))
 
     def constant_terms(tile, b, y_next, y_prior):
         py, pz = wst[tile, 102], wst[tile, 103]

time: 31.6 us -> 31.5 us (level)
  no operation moved by 1% of the time
where the time goes in v4:
time: 31.5 us
  Pallas kernels  30.6 us (97%)
  local copies, waits for them, and re-layouts  0.84 us (3%)
    pallas_call x1, Pallas kernels, on_device(): pl.pallas_call(run, out_shape=jax.ShapeDtypeStruct((5, 4, 4, 2, 8, 128),...  30.6 us
    unnamed x1, local copies, waits for them, and re-layouts  0.84 us

profile of v4, /device:TPU:6, one launch (start us, length us, event | category | flops | bytes accessed | tf_op | source)
XLA Modules:
  0.0 31.5 jit_solution(7856064312988208513)
XLA Ops:
  0.0 30.6 %shard_map.64 = f32[5,4,4,2,8,128]{5,4,3,2,1,0:T(8,128)S(1)} custom-call(f32[5,4,4,2,8,128]{5,4,3,2,1,0:T(8,128)} %bitcast.7, f32[5,5,4,4,2,8,128]{6,5,4,3,2,1,0:T(8,128)} %bitcast.6, f32[75,4,128]{2,1,0:T(4,128)} %bitcast.8, f32[4,128]{1,0:T(4,128)} %refs_3_.1, f32[3,4,128]{2,1,0:T(4,128)} %refs_4_.1, f32[25,4,128]{2,1,0:T(4,128)} %bitcast.9), custom_call_target="tpu_custom_call" | custom-call | tf_op jit(solution)/shard_map/pallas_call | solution.py:844
  30.6 0.8 %copy.8 = f32[5,64,4,128]{3,2,1,0:T(4,128)} copy(f32[5,64,4,128]{3,2,1,0:T(4,128)S(1)} %bitcast.5) | data formatting | bytes 1310720
